TPU v7x, 32 devices: a whole 2x2x4 slice. The times are simulated.
32 devices in a mesh: expert: 8 (over z, core), blk: 4 (over y, x).
Axes of the slice: x: 2, y: 2, z: 4, core: 2. Of those that a mesh axis runs over, the one named last changes fastest.
Arguments:
- tokens: bfloat16 [4096, 3584], P('expert', 'blk'), may hold values from -6 to 6
- route: int32 [4096, 1], P('expert'), may hold values from 0 to 7; in each aligned block of 512 rows (0 to 511, 512 to 1023, ...) at most 96 rows name the same one
- gate_score: float32 [4096, 1], P('expert'), may hold values from 0.1 to 1
- w_gate: bfloat16 [8, 3584, 2048], P('expert', None, 'blk'), may hold values from -0.09375 to 0.09375
- w_up: bfloat16 [8, 3584, 2048], P('expert', None, 'blk'), may hold values from -0.09375 to 0.09375
- w_down: bfloat16 [8, 2048, 3584], P('expert', 'blk'), may hold values from -0.125 to 0.125
Outputs:
- mixed: bfloat16 [4096, 3584], P('expert', 'blk')
Inputs may be any that keep to these rules, and one draw needn't show every extreme that they name: `route`: among the 512 tokens of one index of expert (aligned blocks of rows), no expert is named more than 96 times, a bound that some block reaches.
All inputs are finite; a program needn't handle non-finite values.
Results may differ from a plain program's by a relative error of at most 0.015.
Values may be sent and summed in bfloat16 or wider, within the bound.
No kernel may reach another device: no remote copies, remote signals or barrier semaphores. Data moves between devices by JAX's collectives and lax.ppermute only.
A program may use at most 64 MiB of HBM per device.

v0:
```python
import jax
import jax.numpy as jnp
from jax import lax
from jax.sharding import PartitionSpec as P


def slot_table(route, groups, capacity):
    count = route.shape[0]
    target = route[:, 0]
    later = lax.broadcasted_iota(jnp.int32, (count, count), 0)
    before = lax.broadcasted_iota(jnp.int32, (count, count), 1) < later
    same = target[:, None] == target[None, :]
    rank = jnp.sum(jnp.where(same & before, 1, 0), axis=1).astype(jnp.int32)
    slot_ids = target * capacity + rank
    positions = lax.broadcasted_iota(jnp.int32, (groups * capacity, count), 0)
    return (positions == slot_ids[None, :]).astype(jnp.bfloat16)


def per_device(tokens, route, gate_score, w_gate, w_up, w_down):
    groups = lax.axis_size("expert")
    count = tokens.shape[0]
    capacity = 3 * count // (2 * groups)
    selector = slot_table(route, groups, capacity)
    outgoing = jnp.dot(selector, tokens, preferred_element_type=jnp.float32).astype(jnp.bfloat16)
    arrived = lax.all_to_all(outgoing, "expert", split_axis=0, concat_axis=0, tiled=True)
    gate_rows = w_gate[0]
    up_rows = w_up[0]
    down_rows = w_down[0]
    whole = lax.all_gather(arrived, "blk", axis=1, tiled=True)
    gate_acc = jnp.dot(whole, gate_rows, preferred_element_type=jnp.float32)
    up_acc = jnp.dot(whole, up_rows, preferred_element_type=jnp.float32)
    hidden = (jax.nn.silu(gate_acc) * up_acc).astype(jnp.bfloat16)
    partial_sum = jnp.dot(hidden, down_rows, preferred_element_type=jnp.float32)
    shares = lax.psum_scatter(
        partial_sum.astype(jnp.bfloat16), "blk", scatter_dimension=1, tiled=True
    )
    back = lax.all_to_all(shares, "expert", split_axis=0, concat_axis=0, tiled=True)
    picked = lax.dot_general(
        selector, back, (((0,), (0,)), ((), ())), preferred_element_type=jnp.float32
    )
    return (picked * gate_score).astype(jnp.bfloat16)


def solution(mesh):
    in_specs = (
        P("expert", "blk"),
        P("expert", None),
        P("expert", None),
        P("expert", None, "blk"),
        P("expert", None, "blk"),
        P("expert", "blk", None),
    )
    out_specs = P("expert", "blk")
    return jax.shard_map(
        per_device, mesh=mesh, in_specs=in_specs, out_specs=out_specs, check_vma=False
    )
```

profile of v0, /device:TPU:0, one launch (start us, length us, event | category | flops | bytes accessed | tf_op | source)
XLA Modules:
  0.0 246.9 jit_solution(4046218817611469041)
XLA Ops:
  6.5 0.0 copy-start
  6.5 0.0 all-gather.2.cloned.1.call-start
  6.5 1.0 select_reduce_fusion
  7.6 0.7 multiply_add_fusion
  8.3 0.0 copy-done
  8.3 1.0 convolution_convert_fusion.1
  9.3 39.8 %all_to_all.24 = bf16[8,96,896]{2,1,0:T(8,128)(2,1)} all-to-all(bf16[8,96,896]{2,1,0:T(8,128)(2,1)S(1)} %bitcast.29), channel_id=1, replica_groups=mesh['expert'=8,'blk'=4] {'expert'}, dimensions={0} | all-to-all | bytes 2752512 | tf_op jit(solution)/shard_map/all_to_all | solution.py:25
  49.1 0.0 all-gather.2.cloned.1.call-update
  49.1 0.0 reduce-scatter.4.cloned.1.call-start
  49.2 62.6 %all-gather.2.cloned.1.call-done = bf16[768,3584]{1,0:T(8,128)(2,1)} async-done(((bf16[768,896]{1,0:T(8,128)(2,1)}), bf16[768,3584]{1,0:T(8,128)(2,1)}) %all-gather.2.cloned.1.call-update) | async-done | bytes 5505040 | tf_op jit(solution)/shard_map/all_gather | solution.py:29
  111.8 0.0 copy-start.1
  111.8 0.0 copy-start.2
  111.8 6.2 %fusion.3 = f32[768,512]{1,0:T(8,128)S(1)} fusion(bf16[768,3584]{1,0:T(8,128)(2,1)} %all-gather.2.cloned.1.call-done, bf16[1,3584,512]{2,1,0:T(8,128)(2,1)} %param.9), kind=kOutput, calls=%fused_computation.4 | convolution fusion | flops 2818572288 | bytes 10747904 | tf_op jit(solution)/shard_map/dot_general | solution.py:30
  118.0 0.0 copy-done.1
  118.0 0.1 copy-done.2
  118.2 0.0 copy-start.3
  118.2 3.1 %multiply_convert_fusion.1 = bf16[768,512]{1,0:T(8,128)(2,1)S(1)} fusion(f32[768,512]{1,0:T(8,128)S(1)} %fusion.3, bf16[768,3584]{1,0:T(8,128)(2,1)S(1)} %copy-done.1, bf16[1,3584,512]{2,1,0:T(8,128)(2,1)S(1)} %copy-done.2), kind=kOutput, calls=%fused_computation.8 | convolution fusion | flops 2820931584 | bytes 11534336 | tf_op jit(solution)/shard_map/dot_general | solution.py:31
  121.3 0.0 copy-done.3
  121.3 4.8 %convolution_convert_fusion = bf16[768,3584]{1,0:T(8,128)(2,1)} fusion(bf16[768,512]{1,0:T(8,128)(2,1)S(1)} %multiply_convert_fusion.1, bf16[1,512,3584]{2,1,0:T(8,128)(2,1)S(1)} %copy-done.3), kind=kOutput, calls=%fused_computation | convolution fusion | flops 2821324800 | bytes 9961472 | tf_op jit(solution)/shard_map/dot_general | solution.py:33
  126.1 8.3 %copy.7 = bf16[768,3584]{0,1:T(8,128)(2,1)} copy(bf16[768,3584]{1,0:T(8,128)(2,1)} %convolution_convert_fusion) | data formatting | bytes 11010048
  134.4 0.0 reduce-scatter.4.cloned.1.call-update
  134.5 63.8 %reduce-scatter.4.cloned.1.call-done = bf16[896,768]{1,0:T(8,128)(2,1)} async-done(((bf16[3584,768]{1,0:T(8,128)(2,1)}), bf16[896,768]{1,0:T(8,128)(2,1)}) %reduce-scatter.4.cloned.1.call-update) | async-done | bytes 1376272
  198.2 1.8 copy.8
  200.0 0.0 copy-start.4
  200.0 38.0 %all_to_all.25 = bf16[8,96,896]{2,1,0:T(8,128)(2,1)S(1)} all-to-all(bf16[8,96,896]{2,1,0:T(8,128)(2,1)S(1)} %bitcast.26), channel_id=1, replica_groups=mesh['expert'=8,'blk'=4] {'expert'}, dimensions={0} | all-to-all | bytes 2752512 | tf_op jit(solution)/shard_map/all_to_all | solution.py:37
  238.1 0.0 copy-done.4
  238.1 2.0 multiply_convert_fusion
Async XLA Ops:
  6.5 1.7 copy-start
  6.5 105.3 %all-gather.2.cloned.1.call-start = ((), (), s32[]{:S(2)}) async-start(), calls=%async_computation.3 | async-start | bytes 6881280 | tf_op jit(solution)/shard_map/all_gather | solution.py:29
  49.1 149.1 %reduce-scatter.4.cloned.1.call-start = ((), (), s32[]{:S(2)}) async-start(), calls=%async_computation.4 | async-start | bytes 6881280
  111.8 6.2 %copy-start.1 = (bf16[768,3584]{1,0:T(8,128)(2,1)S(1)}, bf16[768,3584]{1,0:T(8,128)(2,1)}, u32[]{:S(2)}) copy-start(bf16[768,3584]{1,0:T(8,128)(2,1)} %all-gather.2.cloned.1.call-done) | copy-start | bytes 16515076
  111.8 6.3 %copy-start.2 = (bf16[1,3584,512]{2,1,0:T(8,128)(2,1)S(1)}, bf16[1,3584,512]{2,1,0:T(8,128)(2,1)}, u32[]{:S(2)}) copy-start(bf16[1,3584,512]{2,1,0:T(8,128)(2,1)} %param.10) | copy-start | bytes 11010052
  118.2 3.2 %copy-start.3 = (bf16[1,512,3584]{2,1,0:T(8,128)(2,1)S(1)}, bf16[1,512,3584]{2,1,0:T(8,128)(2,1)}, u32[]{:S(2)}) copy-start(bf16[1,512,3584]{2,1,0:T(8,128)(2,1)} %param.11) | copy-start | bytes 11010052
  200.0 38.0 %copy-start.4 = (f32[512,1]{0,1:T(1,128)S(1)}, f32[512,1]{0,1:T(1,128)}, u32[]{:S(2)}) copy-start(f32[512,1]{0,1:T(1,128)} %param.8) | copy-start | bytes 6148
Sparse Core Ops, SparseCore 0:
  49.3 62.5 all-gather.1
  134.6 63.6 reduce-scatter.3
where the time goes:
time: 247 us
  waiting for transfers between devices  126 us (51%)
  blocking collectives  77.9 us (32%)
  matrix products  17.1 us (7%)
  between operations  13.5 us (5%)
  local copies, waits for them, and re-layouts  10.2 us (4%)
    unnamed x3, waiting for transfers between devices  63.8 us
    all_gather x1, waiting for transfers between devices, per_device(): whole = lax.all_gather(arrived, 'blk', axis=1, tiled=True)  62.6 us
    all_to_all x1, blocking collectives, per_device(): lax.all_to_all(outgoing, 'expert', split_axis=0, concat_axis=0, tiled=True)  39.8 us
    all_to_all x1, blocking collectives, per_device(): lax.all_to_all(shares, 'expert', split_axis=0, concat_axis=0, tiled=True)  38 us
    unnamed x12, local copies, waits for them, and re-layouts  10.2 us
    dot_general x1, matrix products, per_device(): gate_acc = jnp.dot(whole, gate_rows, preferred_element_type=jnp.float32)  6.2 us
  transfers between devices with their start and end apart: 2, of which 2 were waited for; matrix products, arithmetic and copies ran while one was open for 0% of the time, Pallas kernels for 0%

commit v1 on v0

v1 whole, which is shorter than its diff:
```python
import functools
import jax
import jax.numpy as jnp
from jax import lax
from jax.experimental import pallas as pl
from jax.experimental.pallas import tpu as pltpu
from jax.sharding import PartitionSpec as P


def slot_ids_of(route):
    count = route.shape[0]
    target = route[:, 0]
    later = lax.broadcasted_iota(jnp.int32, (count, count), 0)
    before = lax.broadcasted_iota(jnp.int32, (count, count), 1) < later
    same = target[:, None] == target[None, :]
    rank = jnp.sum(jnp.where(same & before, 1, 0), axis=1).astype(jnp.int32)
    return target, rank


def selector_of(target, rank, groups, first, slots):
    inside = (rank >= first) & (rank < first + slots)
    ids = jnp.where(inside, target * slots + rank - first, -1)
    positions = lax.broadcasted_iota(jnp.int32, (groups * slots, target.shape[0]), 0)
    return (positions == ids[None, :]).astype(jnp.bfloat16)


def ffn_kernel(me, x0, x1, x2, x3a, x3b, wg, wu, wd, p0, p1, p2, p3a, p3b, gate, up, hidden):
    step = pl.program_id(0)
    half = x3a.shape[0]

    def add(rows, x, first):
        g = jnp.dot(x[...], wg[0], preferred_element_type=jnp.float32)
        u = jnp.dot(x[...], wu[0], preferred_element_type=jnp.float32)
        if first:
            gate[rows, :] = g
            up[rows, :] = u
        else:
            gate[rows, :] += g
            up[rows, :] += u

    whole, top, bottom = slice(None), slice(0, half), slice(half, None)

    @pl.when(step == 0)
    def _():
        add(whole, x0, True)

    @pl.when(step == 1)
    def _():
        add(whole, x1, False)

    @pl.when(step == 2)
    def _():
        add(whole, x2, False)

    @pl.when(step == 3)
    def _():
        add(top, x3a, False)
        add(bottom, x3b, False)
        v = gate[...]
        hidden[...] = (v / (1.0 + jnp.exp(-v)) * up[...]).astype(jnp.bfloat16)

    def part():
        return jnp.dot(hidden[...], wd[...], preferred_element_type=jnp.float32).astype(jnp.bfloat16)

    @pl.when(step == 4)
    def _():
        p = part()
        p3a[...] = p[:half]
        p3b[...] = p[half:]

    @pl.when(step == 5)
    def _():
        p2[...] = part()

    @pl.when(step == 6)
    def _():
        p1[...] = part()

    @pl.when(step == 7)
    def _():
        p0[...] = part()


def ffn(me, x0, x1, x2, x3a, x3b, wg, wu, wd):
    rows, width = x0.shape
    half = rows // 2
    hid = wg.shape[-1]
    n = wg.shape[0]
    full = lambda r: pl.BlockSpec((r, width), lambda j, me: (0, 0))
    w_in = pl.BlockSpec((1, width, hid), lambda j, me: (me[0] ^ jnp.minimum(j, n - 1), 0, 0))
    w_out = pl.BlockSpec((hid, width), lambda j, me: (0, me[0] ^ (2 * n - 1 - jnp.maximum(j, n))))
    sds = lambda r: jax.ShapeDtypeStruct((r, width), jnp.bfloat16)
    return pl.pallas_call(
        ffn_kernel,
        grid_spec=pltpu.PrefetchScalarGridSpec(
            num_scalar_prefetch=1,
            grid=(2 * n,),
            in_specs=[full(rows)] * 3 + [full(half)] * 2 + [w_in, w_in, w_out],
            out_specs=[full(rows)] * 3 + [full(half)] * 2,
            scratch_shapes=[
                pltpu.VMEM((rows, hid), jnp.float32),
                pltpu.VMEM((rows, hid), jnp.float32),
                pltpu.VMEM((rows, hid), jnp.bfloat16),
            ],
        ),
        out_shape=[sds(rows)] * 3 + [sds(half)] * 2,
        compiler_params=pltpu.CompilerParams(vmem_limit_bytes=40 * 1024 * 1024),
        cost_estimate=pl.CostEstimate(
            flops=6 * rows * n * width * hid, bytes_accessed=6 * n * width * hid, transcendentals=rows * hid
        ),
    )(me, x0, x1, x2, x3a, x3b, wg, wu, wd)


def square_layer(arrived, me, wg, wu, wd):
    to_x = [(i, i ^ 1) for i in range(4)]
    to_y = [(i, i ^ 2) for i in range(4)]
    send = lambda a, to: lax.ppermute(a, "blk", to)
    half = arrived.shape[0] // 2
    x1 = send(arrived, to_x)
    x2 = send(arrived, to_y)
    x3a = send(x2[:half], to_x)
    x3b = send(x1[half:], to_y)
    p0, p1, p2, p3a, p3b = ffn(me, arrived, x1, x2, x3a, x3b, wg, wu, wd)
    f32 = lambda a: a.astype(jnp.float32)
    q2a = send(p3a, to_x)
    q1b = send(p3b, to_y)
    p1 = jnp.concatenate([p1[:half], (f32(p1[half:]) + f32(q1b)).astype(jnp.bfloat16)], 0)
    p2 = jnp.concatenate([(f32(p2[:half]) + f32(q2a)).astype(jnp.bfloat16), p2[half:]], 0)
    q0 = send(p1, to_x)
    r0 = send(p2, to_y)
    return (f32(p0) + f32(q0) + f32(r0)).astype(jnp.bfloat16)


def plain_layer(arrived, w_gate, w_up, w_down):
    whole = lax.all_gather(arrived, "blk", axis=1, tiled=True)
    gate_acc = jnp.dot(whole, w_gate, preferred_element_type=jnp.float32)
    up_acc = jnp.dot(whole, w_up, preferred_element_type=jnp.float32)
    hidden = (jax.nn.silu(gate_acc) * up_acc).astype(jnp.bfloat16)
    partial_sum = jnp.dot(hidden, w_down, preferred_element_type=jnp.float32)
    return lax.psum_scatter(partial_sum.astype(jnp.bfloat16), "blk", scatter_dimension=1, tiled=True)


CHUNKS = (1, 1, 1)


def per_device(tokens, route, gate_score, w_gate, w_up, w_down):
    groups = lax.axis_size("expert")
    n = lax.axis_size("blk")
    count, width = tokens.shape
    capacity = 3 * count // (2 * groups)
    target, rank = slot_ids_of(route)
    square = n == 4 and width % 128 == 0
    wg, wu, wd = w_gate[0], w_up[0], w_down[0]
    if square:
        me = lax.axis_index("blk").astype(jnp.int32).reshape(1)
        wg, wu = wg.reshape(n, width, -1), wu.reshape(n, width, -1)
    exchange = lambda a: lax.all_to_all(a, "expert", split_axis=0, concat_axis=0, tiled=True)
    unit = capacity // sum(CHUNKS)
    first, total = 0, None
    for part in CHUNKS:
        slots = unit * part
        selector = selector_of(target, rank, groups, first, slots)
        first += slots
        outgoing = jnp.dot(selector, tokens, preferred_element_type=jnp.float32).astype(jnp.bfloat16)
        arrived = exchange(outgoing)
        shares = square_layer(arrived, me, wg, wu, wd) if square else plain_layer(arrived, wg, wu, wd)
        back = exchange(shares)
        picked = lax.dot_general(selector, back, (((0,), (0,)), ((), ())), preferred_element_type=jnp.float32)
        total = picked if total is None else total + picked
    return (total * gate_score).astype(jnp.bfloat16)


def solution(mesh):
    in_specs = (
        P("expert", "blk"),
        P("expert", None),
        P("expert", None),
        P("expert", None, "blk"),
        P("expert", None, "blk"),
        P("expert", "blk", None),
    )
    return jax.shard_map(
        per_device, mesh=mesh, in_specs=in_specs, out_specs=P("expert", "blk"), check_vma=False
    )
```

time: 247 us -> 199 us (0.81)
  blocking collectives: 77.9 us -> 0 us
  starting transfers between devices: 0.04 us -> 54.4 us
  waiting for transfers between devices: 126 us -> 85.9 us
  Pallas kernels: 0 us -> 24.1 us
  between operations: 13.5 us -> 0.29 us
  other arithmetic: 1.73 us -> 12.5 us
  matrix products: 17.1 us -> 9.96 us
    all_to_all x2 -> x0, blocking collectives: 77.9 us -> none  [the longest x1 39.8 us: per_device(): lax.all_to_all(outgoing, 'expert', split_axis=0, concat_axis=0, tiled=True)]
    unnamed x3 -> x0, waiting for transfers between devices: 63.8 us -> none
    all_gather x1 -> x0, waiting for transfers between devices: 62.6 us -> none  [per_device(): whole = lax.all_gather(arrived, 'blk', axis=1, tiled=True)]
    all_to_all x0 -> x6, waiting for transfers between devices: none -> 52.3 us  [per_device(): lax.all_to_all(a, 'expert', split_axis=0, concat_axis=0, tiled=True)]
    ppermute x0 -> x24, waiting for transfers between devices: none -> 33.6 us  [square_layer(): send = lambda a, to: lax.ppermute(a, 'blk', to)]
    ppermute x0 -> x24, starting transfers between devices: none -> 27.9 us  [square_layer(): send = lambda a, to: lax.ppermute(a, 'blk', to)]
    all_to_all x0 -> x6, starting transfers between devices: none -> 26.5 us  [per_device(): lax.all_to_all(a, 'expert', split_axis=0, concat_axis=0, tiled=True)]
    pallas_call x0 -> x3, Pallas kernels: none -> 24.1 us  [ffn(): pl.pallas_call(ffn_kernel, grid_spec=pltpu.PrefetchScalarGridSpec(num_sca...]
  transfers between devices with their start and end apart: 2 -> 30, of which waited for: 2 -> 10; matrix products, arithmetic and copies ran while one was open for 0% -> 12% of each run, Pallas kernels for 0% -> 12%
where the time goes in v1:
time: 199 us; the launch traced here: 198 us
  waiting for transfers between devices  85.9 us (43%)
  starting transfers between devices  54.4 us (27%)
  Pallas kernels  24.1 us (12%)
  other arithmetic  12.5 us (6%)
  local copies, waits for them, and re-layouts  10.9 us (5%)
  matrix products  9.96 us (5%)
    all_to_all x6, waiting for transfers between devices, per_device(): lax.all_to_all(a, 'expert', split_axis=0, concat_axis=0, tiled=True)  52.3 us
    ppermute x24, waiting for transfers between devices, square_layer(): send = lambda a, to: lax.ppermute(a, 'blk', to)  33.6 us
    ppermute x24, starting transfers between devices, square_layer(): send = lambda a, to: lax.ppermute(a, 'blk', to)  27.9 us
    all_to_all x6, starting transfers between devices, per_device(): lax.all_to_all(a, 'expert', split_axis=0, concat_axis=0, tiled=True)  26.5 us
    pallas_call x3, Pallas kernels, ffn(): pl.pallas_call(ffn_kernel, grid_spec=pltpu.PrefetchScalarGridSpec(num_sca...  24.1 us
    dot_general x3, matrix products, per_device(): lax.dot_general(selector, back, (((0,), (0,)), ((), ())), preferred_eleme...  6.29 us
    convert_element_type x3, other arithmetic, square_layer(): return (f32(p0) + f32(q0) + f32(r0)).astype(jnp.bfloat16)  5 us
    unnamed x26, local copies, waits for them, and re-layouts  4.12 us
  transfers between devices with their start and end apart: 30, of which 10 were waited for; matrix products, arithmetic and copies ran while one was open for 12% of the time, Pallas kernels for 12%

profile of v1, /device:TPU:0, one launch (start us, length us, event | category | flops | bytes accessed | tf_op | source)
XLA Modules:
  0.0 197.9 jit_solution(139412068664500844)
XLA Ops:
  3.0 6.3 %all-to-all-start = ((bf16[8,32,896]{2,1,0:T(8,128)(2,1)}), bf16[8,32,896]{2,1,0:T(8,128)(2,1)S(1)}, u32[]{:S(2)}, u32[]{:S(2)}) async-start(bf16[8,32,896]{2,1,0:T(8,128)(2,1)} %bitcast.2), calls=%async_computation | async-start | bytes 917504 | tf_op jit(solution)/shard_map/all_to_all | solution.py:157
  10.5 12.7 %all-to-all-done = bf16[8,32,896]{2,1,0:T(8,128)(2,1)S(1)} async-done(((bf16[8,32,896]{2,1,0:T(8,128)(2,1)}), bf16[8,32,896]{2,1,0:T(8,128)(2,1)S(1)}, u32[]{:S(2)}, u32[]{:S(2)}) %all-to-all-start) | async-done | bytes 458784 | tf_op jit(solution)/shard_map/all_to_all | solution.py:157
  23.2 3.5 %all-to-all-start.2 = ((bf16[8,32,896]{2,1,0:T(8,128)(2,1)}), bf16[8,32,896]{2,1,0:T(8,128)(2,1)S(1)}, u32[]{:S(2)}, u32[]{:S(2)}) async-start(bf16[8,32,896]{2,1,0:T(8,128)(2,1)} %bitcast.9), calls=%async_computation.2 | async-start | bytes 917504 | tf_op jit(solution)/shard_map/all_to_all | solution.py:157
  27.9 12.7 %all-to-all-done.2 = bf16[8,32,896]{2,1,0:T(8,128)(2,1)S(1)} async-done(((bf16[8,32,896]{2,1,0:T(8,128)(2,1)}), bf16[8,32,896]{2,1,0:T(8,128)(2,1)S(1)}, u32[]{:S(2)}, u32[]{:S(2)}) %all-to-all-start.2) | async-done | bytes 458784 | tf_op jit(solution)/shard_map/all_to_all | solution.py:157
  40.6 3.5 %all-to-all-start.4 = ((bf16[8,32,896]{2,1,0:T(8,128)(2,1)}), bf16[8,32,896]{2,1,0:T(8,128)(2,1)S(1)}, u32[]{:S(2)}, u32[]{:S(2)}) async-start(bf16[8,32,896]{2,1,0:T(8,128)(2,1)} %bitcast.13), calls=%async_computation.4 | async-start | bytes 917504 | tf_op jit(solution)/shard_map/all_to_all | solution.py:157
  44.1 1.6 collective-permute-start.9
  48.2 9.8 %all-to-all-done.4 = bf16[8,32,896]{2,1,0:T(8,128)(2,1)S(1)} async-done(((bf16[8,32,896]{2,1,0:T(8,128)(2,1)}), bf16[8,32,896]{2,1,0:T(8,128)(2,1)S(1)}, u32[]{:S(2)}, u32[]{:S(2)}) %all-to-all-start.4) | async-done | bytes 458784 | tf_op jit(solution)/shard_map/all_to_all | solution.py:157
  61.0 1.6 slice.74
  63.2 1.6 slice.75
  64.8 2.6 %collective-permute-done.1.x2 = bf16[256,896]{1,0:T(8,128)(2,1)} collective-permute-done((bf16[256,896]{1,0:T(8,128)(2,1)S(1)}, bf16[256,896]{1,0:T(8,128)(2,1)}, u32[]{:S(2)}, u32[]{:S(2)}) %collective-permute-start.1) | collective-permute-done | bytes 458784 | tf_op jit(solution)/shard_map/ppermute | solution.py:117
  69.9 1.6 collective-permute-start.2
  72.4 4.7 %collective-permute-done.17.x2 = bf16[256,896]{1,0:T(8,128)(2,1)S(1)} collective-permute-done((bf16[256,896]{1,0:T(8,128)(2,1)S(1)}, bf16[256,896]{1,0:T(8,128)(2,1)S(1)}, u32[]{:S(2)}, u32[]{:S(2)}) %collective-permute-start.17) | collective-permute-done | bytes 458784 | tf_op jit(solution)/shard_map/ppermute | solution.py:117
  80.3 3.3 %collective-permute-done.10.x3a = bf16[128,896]{1,0:T(8,128)(2,1)S(1)} collective-permute-done((bf16[128,896]{1,0:T(8,128)(2,1)}, bf16[128,896]{1,0:T(8,128)(2,1)S(1)}, u32[]{:S(2)}, u32[]{:S(2)}) %collective-permute-start.10) | collective-permute-done | bytes 229408 | tf_op jit(solution)/shard_map/ppermute | solution.py:117
  84.1 2.0 %copy-done.1 = bf16[1,3584,512]{2,1,0:T(8,128)(2,1)S(1)} copy-done((bf16[1,3584,512]{2,1,0:T(8,128)(2,1)S(1)}, bf16[1,3584,512]{2,1,0:T(8,128)(2,1)}, u32[]{:S(2)}) %copy-start.1) | copy-done | bytes 3670040
  86.2 2.0 %copy-done.3 = bf16[1,3584,512]{2,1,0:T(8,128)(2,1)S(1)} copy-done((bf16[1,3584,512]{2,1,0:T(8,128)(2,1)S(1)}, bf16[1,3584,512]{2,1,0:T(8,128)(2,1)}, u32[]{:S(2)}) %copy-start.3) | copy-done | bytes 3670040
  88.2 8.0 %shard_map.65 = (bf16[256,896]{1,0:T(8,128)(2,1)S(1)}, bf16[256,896]{1,0:T(8,128)(2,1)S(1)}, bf16[256,896]{1,0:T(8,128)(2,1)S(1)}, bf16[128,896]{1,0:T(8,128)(2,1)S(1)}, bf16[128,896]{1,0:T(8,128)(2,1)S(1)}) custom-call(s32[1]{0:T(128)} %bitcast.1.me, bf16[256,896]{1,0:T(8,128)(2,1)S(1)} %bitcast.38, bf16[256,896]{1,0:T(8,128)(2,1)} %collective-permute-done.8.x1, ...), custom_call_target="tpu_custom_call" | custom-call | flops 2818572288 | bytes 11010048 | tf_op jit(solution)/shard_map/pallas_call | solution.py:93
  96.3 1.6 collective-permute-start.12
  99.4 7.8 %shard_map.64 = (bf16[256,896]{1,0:T(8,128)(2,1)S(1)}, bf16[256,896]{1,0:T(8,128)(2,1)S(1)}, bf16[256,896]{1,0:T(8,128)(2,1)S(1)}, bf16[128,896]{1,0:T(8,128)(2,1)S(1)}, bf16[128,896]{1,0:T(8,128)(2,1)S(1)}) custom-call(s32[1]{0:T(128)} %bitcast.1.me, bf16[256,896]{1,0:T(8,128)(2,1)S(1)} %bitcast.35, bf16[256,896]{1,0:T(8,128)(2,1)} %collective-permute-done.x1, ...), custom_call_target="tpu_custom_call" | custom-call | flops 2818572288 | bytes 11010048 | tf_op jit(solution)/shard_map/pallas_call | solution.py:93
  108.4 8.2 %shard_map.66 = (bf16[256,896]{1,0:T(8,128)(2,1)S(1)}, bf16[256,896]{1,0:T(8,128)(2,1)S(1)}, bf16[256,896]{1,0:T(8,128)(2,1)S(1)}, bf16[128,896]{1,0:T(8,128)(2,1)}, bf16[128,896]{1,0:T(8,128)(2,1)S(1)}) custom-call(s32[1]{0:T(128)} %bitcast.1.me, bf16[256,896]{1,0:T(8,128)(2,1)S(1)} %bitcast.32, bf16[256,896]{1,0:T(8,128)(2,1)S(1)} %collective-permute-done.16.x1, ...), custom_call_target="tpu_custom_call" | custom-call | flops 2818572288 | bytes 11010048 | tf_op jit(solution)/shard_map/pallas_call | solution.py:93
  125.8 10.6 %collective-permute-done.15 = bf16[256,896]{1,0:T(8,128)(2,1)S(1)} collective-permute-done((bf16[256,896]{1,0:T(8,128)(2,1)S(1)}, bf16[256,896]{1,0:T(8,128)(2,1)S(1)}, u32[]{:S(2)}, u32[]{:S(2)}) %collective-permute-start.15) | collective-permute-done | bytes 458784 | tf_op jit(solution)/shard_map/ppermute | solution.py:117
  138.9 5.0 %all-to-all-start.3 = ((bf16[8,32,896]{2,1,0:T(8,128)(2,1)}), bf16[8,32,896]{2,1,0:T(8,128)(2,1)S(1)}, u32[]{:S(2)}, u32[]{:S(2)}) async-start(bf16[8,32,896]{2,1,0:T(8,128)(2,1)} %bitcast.11), calls=%async_computation.3 | async-start | bytes 917504 | tf_op jit(solution)/shard_map/all_to_all | solution.py:157
  144.9 1.7 pad_maximum_fusion.5
  149.2 2.1 %add_convert_fusion.2 = bf16[256,896]{1,0:T(8,128)(2,1)} fusion(bf16[256,896]{1,0:T(8,128)(2,1)} %collective-permute-done.7, bf16[256,896]{1,0:T(8,128)(2,1)} %collective-permute-done.5, bf16[256,896]{1,0:T(8,128)(2,1)S(1)} %get-tuple-element.20), kind=kLoop, calls=%fused_computation.9 | loop fusion | flops 1376256 | bytes 1835008 | tf_op jit(solution)/shard_map/convert_element_type | solution.py:131
  151.3 6.6 %all-to-all-done.3 = bf16[8,32,896]{2,1,0:T(8,128)(2,1)S(1)} async-done(((bf16[8,32,896]{2,1,0:T(8,128)(2,1)}), bf16[8,32,896]{2,1,0:T(8,128)(2,1)S(1)}, u32[]{:S(2)}, u32[]{:S(2)}) %all-to-all-start.3) | async-done | bytes 458784 | tf_op jit(solution)/shard_map/all_to_all | solution.py:157
  157.8 3.5 %all-to-all-start.1 = ((bf16[8,32,896]{2,1,0:T(8,128)(2,1)}), bf16[8,32,896]{2,1,0:T(8,128)(2,1)S(1)}, u32[]{:S(2)}, u32[]{:S(2)}) async-start(bf16[8,32,896]{2,1,0:T(8,128)(2,1)} %bitcast.7), calls=%async_computation.1 | async-start | bytes 917504 | tf_op jit(solution)/shard_map/all_to_all | solution.py:157
  162.0 12.2 %collective-permute-done.21 = bf16[256,896]{1,0:T(8,128)(2,1)S(1)} collective-permute-done((bf16[256,896]{1,0:T(8,128)(2,1)S(1)}, bf16[256,896]{1,0:T(8,128)(2,1)S(1)}, u32[]{:S(2)}, u32[]{:S(2)}) %collective-permute-start.21) | collective-permute-done | bytes 458784 | tf_op jit(solution)/shard_map/ppermute | solution.py:117
  174.3 2.0 add_convert_fusion
  176.2 4.8 %all-to-all-start.5 = ((bf16[8,32,896]{2,1,0:T(8,128)(2,1)}), bf16[8,32,896]{2,1,0:T(8,128)(2,1)S(1)}, u32[]{:S(2)}, u32[]{:S(2)}) async-start(bf16[8,32,896]{2,1,0:T(8,128)(2,1)} %bitcast.15), calls=%async_computation.5 | async-start | bytes 917504 | tf_op jit(solution)/shard_map/all_to_all | solution.py:157
  181.1 1.6 fusion.2
  182.6 1.8 fusion.1
  184.4 10.6 %all-to-all-done.5 = bf16[8,32,896]{2,1,0:T(8,128)(2,1)S(1)} async-done(((bf16[8,32,896]{2,1,0:T(8,128)(2,1)}), bf16[8,32,896]{2,1,0:T(8,128)(2,1)S(1)}, u32[]{:S(2)}, u32[]{:S(2)}) %all-to-all-start.5) | async-done | bytes 458784 | tf_op jit(solution)/shard_map/all_to_all | solution.py:157
  195.0 3.0 %multiply_convert_fusion = bf16[512,896]{1,0:T(8,128)(2,1)} fusion(f32[512,896]{1,0:T(8,128)S(1)} %fusion.2, f32[512,896]{1,0:T(8,128)} %fusion.1, bf16[256,896]{1,0:T(8,128)(2,1)S(1)} %bitcast.42, f32[512]{0:T(512)S(1)} %bitcast.47, s32[512]{0:T(512)S(1)} %get-tuple-element.35), kind=kOutput, calls=%fused_computation | convolution fusion | flops 236847104 | bytes 5050368 | tf_op jit(solution)/shard_map/dot_general | solution.py:168
  (92 shorter events, 37.0 us)
Async XLA Ops:
  3.0 20.3 %all-to-all-start = ((bf16[8,32,896]{2,1,0:T(8,128)(2,1)}), bf16[8,32,896]{2,1,0:T(8,128)(2,1)S(1)}, u32[]{:S(2)}, u32[]{:S(2)}) async-start(bf16[8,32,896]{2,1,0:T(8,128)(2,1)} %bitcast.2), calls=%async_computation | async-start | bytes 917504 | tf_op jit(solution)/shard_map/all_to_all | solution.py:157
  23.2 17.4 %all-to-all-start.2 = ((bf16[8,32,896]{2,1,0:T(8,128)(2,1)}), bf16[8,32,896]{2,1,0:T(8,128)(2,1)S(1)}, u32[]{:S(2)}, u32[]{:S(2)}) async-start(bf16[8,32,896]{2,1,0:T(8,128)(2,1)} %bitcast.9), calls=%async_computation.2 | async-start | bytes 917504 | tf_op jit(solution)/shard_map/all_to_all | solution.py:157
  40.6 17.4 %all-to-all-start.4 = ((bf16[8,32,896]{2,1,0:T(8,128)(2,1)}), bf16[8,32,896]{2,1,0:T(8,128)(2,1)S(1)}, u32[]{:S(2)}, u32[]{:S(2)}) async-start(bf16[8,32,896]{2,1,0:T(8,128)(2,1)} %bitcast.13), calls=%async_computation.4 | async-start | bytes 917504 | tf_op jit(solution)/shard_map/all_to_all | solution.py:157
  44.1 15.4 %collective-permute-start.9 = (bf16[256,896]{1,0:T(8,128)(2,1)S(1)}, bf16[256,896]{1,0:T(8,128)(2,1)}, u32[]{:S(2)}, u32[]{:S(2)}) collective-permute-start(bf16[256,896]{1,0:T(8,128)(2,1)S(1)} %bitcast.36), channel_id=1, source_target_pairs={{0,2},{1,3},{2,0},{3,1},{4,6},{5,7},{6,4},{7,5},{8,10},{9,11},{10,... | collective-permute-start | bytes 1376264 | tf_op jit(solution)/shard_map/ppermute | solution.py:117
  45.7 17.0 %collective-permute-start.8 = (bf16[256,896]{1,0:T(8,128)(2,1)S(1)}, bf16[256,896]{1,0:T(8,128)(2,1)}, u32[]{:S(2)}, u32[]{:S(2)}) collective-permute-start(bf16[256,896]{1,0:T(8,128)(2,1)S(1)} %bitcast.37), channel_id=1, source_target_pairs={{0,1},{1,0},{2,3},{3,2},{4,5},{5,4},{6,7},{7,6},{8,9},{9,8},{10,11... | collective-permute-start | bytes 1376264 | tf_op jit(solution)/shard_map/ppermute | solution.py:117
  47.2 20.3 %collective-permute-start.1 = (bf16[256,896]{1,0:T(8,128)(2,1)S(1)}, bf16[256,896]{1,0:T(8,128)(2,1)}, u32[]{:S(2)}, u32[]{:S(2)}) collective-permute-start(bf16[256,896]{1,0:T(8,128)(2,1)S(1)} %bitcast.33), channel_id=1, source_target_pairs={{0,2},{1,3},{2,0},{3,1},{4,6},{5,7},{6,4},{7,5},{8,10},{9,11},{10,... | collective-permute-start | bytes 1376264 | tf_op jit(solution)/shard_map/ppermute | solution.py:117
  47.7 22.2 %collective-permute-start = (bf16[256,896]{1,0:T(8,128)(2,1)S(1)}, bf16[256,896]{1,0:T(8,128)(2,1)}, u32[]{:S(2)}, u32[]{:S(2)}) collective-permute-start(bf16[256,896]{1,0:T(8,128)(2,1)S(1)} %bitcast.34), channel_id=1, source_target_pairs={{0,1},{1,0},{2,3},{3,2},{4,5},{5,4},{6,7},{7,6},{8,9},{9,8},{10,11... | collective-permute-start | bytes 1376264 | tf_op jit(solution)/shard_map/ppermute | solution.py:117
  58.0 19.2 %collective-permute-start.17 = (bf16[256,896]{1,0:T(8,128)(2,1)S(1)}, bf16[256,896]{1,0:T(8,128)(2,1)S(1)}, u32[]{:S(2)}, u32[]{:S(2)}) collective-permute-start(bf16[256,896]{1,0:T(8,128)(2,1)S(1)} %bitcast.30), channel_id=1, source_target_pairs={{0,2},{1,3},{2,0},{3,1},{4,6},{5,7},{6,4},{7,5},{8,10},{9,11},{10,... | collective-permute-start | bytes 1376264 | tf_op jit(solution)/shard_map/ppermute | solution.py:117
  59.5 19.2 %collective-permute-start.16 = (bf16[256,896]{1,0:T(8,128)(2,1)S(1)}, bf16[256,896]{1,0:T(8,128)(2,1)S(1)}, u32[]{:S(2)}, u32[]{:S(2)}) collective-permute-start(bf16[256,896]{1,0:T(8,128)(2,1)S(1)} %bitcast.31), channel_id=1, source_target_pairs={{0,1},{1,0},{2,3},{3,2},{4,5},{5,4},{6,7},{7,6},{8,9},{9,8},{10,11... | collective-permute-start | bytes 1376264 | tf_op jit(solution)/shard_map/ppermute | solution.py:117
  62.6 21.0 %collective-permute-start.10 = (bf16[128,896]{1,0:T(8,128)(2,1)}, bf16[128,896]{1,0:T(8,128)(2,1)S(1)}, u32[]{:S(2)}, u32[]{:S(2)}) collective-permute-start(bf16[128,896]{1,0:T(8,128)(2,1)} %slice.74), channel_id=1, source_target_pairs={{0,1},{1,0},{2,3},{3,2},{4,5},{5,4},{6,7},{7,6},{8,9},{9,8},{10,11... | collective-permute-start | bytes 688136 | tf_op jit(solution)/shard_map/ppermute | solution.py:117
  67.4 16.7 %collective-permute-start.11 = (bf16[128,896]{1,0:T(8,128)(2,1)}, bf16[128,896]{1,0:T(8,128)(2,1)}, u32[]{:S(2)}, u32[]{:S(2)}) collective-permute-start(bf16[128,896]{1,0:T(8,128)(2,1)} %slice.75), channel_id=1, source_target_pairs={{0,2},{1,3},{2,0},{3,1},{4,6},{5,7},{6,4},{7,5},{8,10},{9,11},{10,... | collective-permute-start | bytes 688136 | tf_op jit(solution)/shard_map/ppermute | solution.py:117
  69.9 28.0 %collective-permute-start.2 = (bf16[128,896]{1,0:T(8,128)(2,1)S(1)}, bf16[128,896]{1,0:T(8,128)(2,1)S(1)}, u32[]{:S(2)}, u32[]{:S(2)}) collective-permute-start(bf16[128,896]{1,0:T(8,128)(2,1)S(1)} %slice.72), channel_id=1, source_target_pairs={{0,1},{1,0},{2,3},{3,2},{4,5},{5,4},{6,7},{7,6},{8,9},{9,8},{10,11... | collective-permute-start | bytes 688136 | tf_op jit(solution)/shard_map/ppermute | solution.py:117
  77.2 22.2 %collective-permute-start.3 = (bf16[128,896]{1,0:T(8,128)(2,1)S(1)}, bf16[128,896]{1,0:T(8,128)(2,1)S(1)}, u32[]{:S(2)}, u32[]{:S(2)}) collective-permute-start(bf16[128,896]{1,0:T(8,128)(2,1)S(1)} %slice.73), channel_id=1, source_target_pairs={{0,2},{1,3},{2,0},{3,1},{4,6},{5,7},{6,4},{7,5},{8,10},{9,11},{10,... | collective-permute-start | bytes 688136 | tf_op jit(solution)/shard_map/ppermute | solution.py:117
  78.7 29.2 %collective-permute-start.18 = (bf16[128,896]{1,0:T(8,128)(2,1)S(1)}, bf16[128,896]{1,0:T(8,128)(2,1)S(1)}, u32[]{:S(2)}, u32[]{:S(2)}) collective-permute-start(bf16[128,896]{1,0:T(8,128)(2,1)S(1)} %slice.76), channel_id=1, source_target_pairs={{0,1},{1,0},{2,3},{3,2},{4,5},{5,4},{6,7},{7,6},{8,9},{9,8},{10,11... | collective-permute-start | bytes 688136 | tf_op jit(solution)/shard_map/ppermute | solution.py:117
  83.6 24.8 %collective-permute-start.19 = (bf16[128,896]{1,0:T(8,128)(2,1)S(1)}, bf16[128,896]{1,0:T(8,128)(2,1)S(1)}, u32[]{:S(2)}, u32[]{:S(2)}) collective-permute-start(bf16[128,896]{1,0:T(8,128)(2,1)S(1)} %slice.77), channel_id=1, source_target_pairs={{0,2},{1,3},{2,0},{3,1},{4,6},{5,7},{6,4},{7,5},{8,10},{9,11},{10,... | collective-permute-start | bytes 688136 | tf_op jit(solution)/shard_map/ppermute | solution.py:117
  96.3 24.9 %collective-permute-start.12 = (bf16[128,896]{1,0:T(8,128)(2,1)S(1)}, bf16[128,896]{1,0:T(8,128)(2,1)S(1)}, u32[]{:S(2)}, u32[]{:S(2)}) collective-permute-start(bf16[128,896]{1,0:T(8,128)(2,1)S(1)} %get-tuple-element.27), channel_id=1, source_target_pairs={{0,2},{1,3},{2,0},{3,1},{4,6},{5,7},{6,4},{7,5},{8,10},{9,11},{10,... | collective-permute-start | bytes 688136 | tf_op jit(solution)/shard_map/ppermute | solution.py:117
  97.9 21.7 %collective-permute-start.14 = (bf16[128,896]{1,0:T(8,128)(2,1)S(1)}, bf16[128,896]{1,0:T(8,128)(2,1)S(1)}, u32[]{:S(2)}, u32[]{:S(2)}) collective-permute-start(bf16[128,896]{1,0:T(8,128)(2,1)S(1)} %get-tuple-element.29), channel_id=1, source_target_pairs={{0,1},{1,0},{2,3},{3,2},{4,5},{5,4},{6,7},{7,6},{8,9},{9,8},{10,11... | collective-permute-start | bytes 688136 | tf_op jit(solution)/shard_map/ppermute | solution.py:117
  107.3 16.1 %collective-permute-start.4 = (bf16[128,896]{1,0:T(8,128)(2,1)S(1)}, bf16[128,896]{1,0:T(8,128)(2,1)S(1)}, u32[]{:S(2)}, u32[]{:S(2)}) collective-permute-start(bf16[128,896]{1,0:T(8,128)(2,1)S(1)} %get-tuple-element.22), channel_id=1, source_target_pairs={{0,2},{1,3},{2,0},{3,1},{4,6},{5,7},{6,4},{7,5},{8,10},{9,11},{10,... | collective-permute-start | bytes 688136 | tf_op jit(solution)/shard_map/ppermute | solution.py:117
  107.9 14.0 %collective-permute-start.6 = (bf16[128,896]{1,0:T(8,128)(2,1)S(1)}, bf16[128,896]{1,0:T(8,128)(2,1)S(1)}, u32[]{:S(2)}, u32[]{:S(2)}) collective-permute-start(bf16[128,896]{1,0:T(8,128)(2,1)S(1)} %get-tuple-element.24), channel_id=1, source_target_pairs={{0,1},{1,0},{2,3},{3,2},{4,5},{5,4},{6,7},{7,6},{8,9},{9,8},{10,11... | collective-permute-start | bytes 688136 | tf_op jit(solution)/shard_map/ppermute | solution.py:117
  118.1 30.1 %collective-permute-start.20 = (bf16[128,896]{1,0:T(8,128)(2,1)S(1)}, bf16[128,896]{1,0:T(8,128)(2,1)}, u32[]{:S(2)}, u32[]{:S(2)}) collective-permute-start(bf16[128,896]{1,0:T(8,128)(2,1)S(1)} %get-tuple-element.32), channel_id=1, source_target_pairs={{0,2},{1,3},{2,0},{3,1},{4,6},{5,7},{6,4},{7,5},{8,10},{9,11},{10,... | collective-permute-start | bytes 688136 | tf_op jit(solution)/shard_map/ppermute | solution.py:117
  119.6 24.3 %collective-permute-start.22 = (bf16[128,896]{1,0:T(8,128)(2,1)}, bf16[128,896]{1,0:T(8,128)(2,1)}, u32[]{:S(2)}, u32[]{:S(2)}) collective-permute-start(bf16[128,896]{1,0:T(8,128)(2,1)} %get-tuple-element.34), channel_id=1, source_target_pairs={{0,1},{1,0},{2,3},{3,2},{4,5},{5,4},{6,7},{7,6},{8,9},{9,8},{10,11... | collective-permute-start | bytes 688136 | tf_op jit(solution)/shard_map/ppermute | solution.py:117
  121.2 15.2 %collective-permute-start.15 = (bf16[256,896]{1,0:T(8,128)(2,1)S(1)}, bf16[256,896]{1,0:T(8,128)(2,1)S(1)}, u32[]{:S(2)}, u32[]{:S(2)}) collective-permute-start(bf16[256,896]{1,0:T(8,128)(2,1)S(1)} %pad_maximum_fusion.3), channel_id=1, source_target_pairs={{0,2},{1,3},{2,0},{3,1},{4,6},{5,7},{6,4},{7,5},{8,10},{9,11},{10,... | collective-permute-start | bytes 1376264 | tf_op jit(solution)/shard_map/ppermute | solution.py:117
  121.9 16.0 %collective-permute-start.13 = (bf16[256,896]{1,0:T(8,128)(2,1)S(1)}, bf16[256,896]{1,0:T(8,128)(2,1)S(1)}, u32[]{:S(2)}, u32[]{:S(2)}) collective-permute-start(bf16[256,896]{1,0:T(8,128)(2,1)S(1)} %pad_maximum_fusion.2), channel_id=1, source_target_pairs={{0,1},{1,0},{2,3},{3,2},{4,5},{5,4},{6,7},{7,6},{8,9},{9,8},{10,11... | collective-permute-start | bytes 1376264 | tf_op jit(solution)/shard_map/ppermute | solution.py:117
  123.4 25.8 %collective-permute-start.7 = (bf16[256,896]{1,0:T(8,128)(2,1)}, bf16[256,896]{1,0:T(8,128)(2,1)}, u32[]{:S(2)}, u32[]{:S(2)}) collective-permute-start(bf16[256,896]{1,0:T(8,128)(2,1)} %pad_maximum_fusion.1), channel_id=1, source_target_pairs={{0,2},{1,3},{2,0},{3,1},{4,6},{5,7},{6,4},{7,5},{8,10},{9,11},{10,... | collective-permute-start | bytes 1376264 | tf_op jit(solution)/shard_map/ppermute | solution.py:117
  125.0 18.9 %copy-start.7 = (bf16[256,896]{1,0:T(8,128)(2,1)S(1)}, bf16[256,896]{1,0:T(8,128)(2,1)}, u32[]{:S(2)}) copy-start(bf16[256,896]{1,0:T(8,128)(2,1)} %copy-done.6) | copy-start | bytes 1376260
  136.4 12.8 %collective-permute-start.5 = (bf16[256,896]{1,0:T(8,128)(2,1)}, bf16[256,896]{1,0:T(8,128)(2,1)}, u32[]{:S(2)}, u32[]{:S(2)}) collective-permute-start(bf16[256,896]{1,0:T(8,128)(2,1)} %pad_maximum_fusion), channel_id=1, source_target_pairs={{0,1},{1,0},{2,3},{3,2},{4,5},{5,4},{6,7},{7,6},{8,9},{9,8},{10,11... | collective-permute-start | bytes 1376264 | tf_op jit(solution)/shard_map/ppermute | solution.py:117
  138.9 18.9 %all-to-all-start.3 = ((bf16[8,32,896]{2,1,0:T(8,128)(2,1)}), bf16[8,32,896]{2,1,0:T(8,128)(2,1)S(1)}, u32[]{:S(2)}, u32[]{:S(2)}) async-start(bf16[8,32,896]{2,1,0:T(8,128)(2,1)} %bitcast.11), calls=%async_computation.3 | async-start | bytes 917504 | tf_op jit(solution)/shard_map/all_to_all | solution.py:157
  146.6 15.4 %collective-permute-start.23 = (bf16[256,896]{1,0:T(8,128)(2,1)}, bf16[256,896]{1,0:T(8,128)(2,1)}, u32[]{:S(2)}, u32[]{:S(2)}) collective-permute-start(bf16[256,896]{1,0:T(8,128)(2,1)} %pad_maximum_fusion.5), channel_id=1, source_target_pairs={{0,2},{1,3},{2,0},{3,1},{4,6},{5,7},{6,4},{7,5},{8,10},{9,11},{10,... | collective-permute-start | bytes 1376264 | tf_op jit(solution)/shard_map/ppermute | solution.py:117
  157.8 18.4 %copy-start.8 = (bf16[8,32,896]{2,1,0:T(8,128)(2,1)}, bf16[8,32,896]{2,1,0:T(8,128)(2,1)S(1)}, u32[]{:S(2)}) copy-start(bf16[8,32,896]{2,1,0:T(8,128)(2,1)S(1)} %all-to-all-done.3) | copy-start | bytes 1376260
  157.8 18.4 %all-to-all-start.1 = ((bf16[8,32,896]{2,1,0:T(8,128)(2,1)}), bf16[8,32,896]{2,1,0:T(8,128)(2,1)S(1)}, u32[]{:S(2)}, u32[]{:S(2)}) async-start(bf16[8,32,896]{2,1,0:T(8,128)(2,1)} %bitcast.7), calls=%async_computation.1 | async-start | bytes 917504 | tf_op jit(solution)/shard_map/all_to_all | solution.py:157
  161.4 12.9 %collective-permute-start.21 = (bf16[256,896]{1,0:T(8,128)(2,1)S(1)}, bf16[256,896]{1,0:T(8,128)(2,1)S(1)}, u32[]{:S(2)}, u32[]{:S(2)}) collective-permute-start(bf16[256,896]{1,0:T(8,128)(2,1)S(1)} %pad_maximum_fusion.4), channel_id=1, source_target_pairs={{0,1},{1,0},{2,3},{3,2},{4,5},{5,4},{6,7},{7,6},{8,9},{9,8},{10,11... | collective-permute-start | bytes 1376264 | tf_op jit(solution)/shard_map/ppermute | solution.py:117
  176.2 18.7 %all-to-all-start.5 = ((bf16[8,32,896]{2,1,0:T(8,128)(2,1)}), bf16[8,32,896]{2,1,0:T(8,128)(2,1)S(1)}, u32[]{:S(2)}, u32[]{:S(2)}) async-start(bf16[8,32,896]{2,1,0:T(8,128)(2,1)} %bitcast.15), calls=%async_computation.5 | async-start | bytes 917504 | tf_op jit(solution)/shard_map/all_to_all | solution.py:157
  (11 other events, 72.7 us)

commit v2 on v0

v2 whole, which is shorter than its diff:
```python
import jax
import jax.numpy as jnp
from jax import lax
from jax.experimental import pallas as pl
from jax.experimental.pallas import tpu as pltpu
from jax.sharding import PartitionSpec as P

RING = (0, 1, 3, 2)


def rank_of(target):
    count = target.shape[0]
    later = lax.broadcasted_iota(jnp.int32, (count, count), 0)
    before = lax.broadcasted_iota(jnp.int32, (count, count), 1) < later
    same = target[:, None] == target[None, :]
    return jnp.sum(jnp.where(same & before, 1, 0), axis=1).astype(jnp.int32)


def selector_of(slot_ids, slots):
    positions = lax.broadcasted_iota(jnp.int32, (slots, slot_ids.shape[0]), 0)
    return (positions == slot_ids[None, :]).astype(jnp.bfloat16)


def hidden_kernel(order, x0, x1, x2, x3, wg, wu, wd, hidden, part):
    width = x0.shape[1]
    gate = up = None
    for j, x in enumerate((x0, x1, x2, x3)):
        rows = pl.ds(pl.multiple_of(order[j] * width, width), width)
        g = jnp.dot(x[...], wg[rows, :], preferred_element_type=jnp.float32)
        u = jnp.dot(x[...], wu[rows, :], preferred_element_type=jnp.float32)
        gate, up = (g, u) if gate is None else (gate + g, up + u)
    hidden[...] = (gate / (1.0 + jnp.exp(-gate)) * up).astype(jnp.bfloat16)
    cols = pl.ds(pl.multiple_of(order[1] * width, width), width)
    part[...] = jnp.dot(hidden[...], wd[:, cols], preferred_element_type=jnp.float32).astype(jnp.bfloat16)


def down_kernel(j, order, hidden, arrived, wd, out):
    width = out.shape[1]
    cols = pl.ds(pl.multiple_of(order[j] * width, width), width)
    part = jnp.dot(hidden[...], wd[:, cols], preferred_element_type=jnp.float32)
    out[...] = (part + arrived[...].astype(jnp.float32)).astype(jnp.bfloat16)


SMEM = pl.BlockSpec(memory_space=pltpu.SMEM)
VMEM = pl.BlockSpec(memory_space=pltpu.VMEM)
LIMIT = pltpu.CompilerParams(vmem_limit_bytes=32 * 1024 * 1024)


def hidden_of(order, xs, wg, wu, wd):
    rows, width = xs[0].shape
    hid = wg.shape[1]
    n = len(xs)
    return pl.pallas_call(
        hidden_kernel,
        in_specs=[SMEM] + [VMEM] * 7,
        out_specs=[VMEM] * 2,
        out_shape=[
            jax.ShapeDtypeStruct((rows, hid), jnp.bfloat16),
            jax.ShapeDtypeStruct((rows, width), jnp.bfloat16),
        ],
        compiler_params=LIMIT,
        cost_estimate=pl.CostEstimate(
            flops=2 * rows * width * hid * (2 * n + 1), bytes_accessed=6 * n * width * hid, transcendentals=rows * hid
        ),
    )(order, *xs, wg, wu, wd)


def down_of(j, order, hidden, arrived, wd):
    rows, hid = hidden.shape
    width = arrived.shape[1]
    return pl.pallas_call(
        lambda *refs: down_kernel(j, *refs),
        in_specs=[SMEM] + [VMEM] * 3,
        out_specs=VMEM,
        out_shape=jax.ShapeDtypeStruct((rows, width), jnp.bfloat16),
        compiler_params=LIMIT,
        cost_estimate=pl.CostEstimate(
            flops=2 * rows * width * hid, bytes_accessed=2 * width * hid + 4 * rows * width, transcendentals=0
        ),
    )(order, hidden, arrived, wd)


def ring_perm(groups, n):
    pairs = []
    for e in range(groups):
        for i in range(n):
            here, there = RING[i], RING[(i + (1 if e % 2 == 0 else -1)) % n]
            pairs.append((e * n + here, e * n + there))
    return pairs


def ring_layer(held, order, perm, wg, wu, wd):
    step = lambda a: lax.ppermute(a, ("expert", "blk"), perm)
    xs = [held]
    for _ in range(3):
        xs.append(step(xs[-1]))
    hidden, part = hidden_of(order, xs, wg, wu, wd)
    for j in (2, 3, 0):
        part = down_of(j, order, hidden, step(part), wd)
    return part


def square_program(tokens, route, gate_score, wg, wu, wd, capacity):
    groups, n = lax.axis_size("expert"), lax.axis_size("blk")
    me, place = lax.axis_index("expert"), lax.axis_index("blk")
    target = route[:, 0]
    relative = target ^ me
    slot_ids = relative * capacity + rank_of(target)
    selector = selector_of(slot_ids, groups * capacity)
    outgoing = jnp.dot(selector, tokens, preferred_element_type=jnp.float32).astype(jnp.bfloat16)
    chunks, width = groups // 2, tokens.shape[1]
    outgoing = outgoing.reshape(chunks, 2, capacity, width)
    sibling = lambda a: lax.ppermute(a, "expert", [(i, i ^ 1) for i in range(groups)])
    other = lambda a, k: lax.ppermute(a, "expert", [(i, i ^ (2 * k)) for i in range(groups)]) if k else a
    swapped = sibling(outgoing[:, 1])
    perm = ring_perm(groups, n)
    forward = {RING[i]: [RING[(i - s) % n] for s in range(n)] for i in range(n)}
    backward = {RING[i]: [RING[(i + s) % n] for s in range(n)] for i in range(n)}
    table = jnp.array([[forward[i] for i in range(n)], [backward[i] for i in range(n)]], jnp.int32)
    order = table[me % 2, place]
    backs = [None] * chunks
    for k in range(chunks):
        chunk = jnp.concatenate([outgoing[k, 0], swapped[k]], 0)
        shares = ring_layer(other(chunk, k), order, perm, wg, wu, wd)
        backs[k] = other(shares, k).reshape(2, capacity, width)
    own = jnp.stack([b[0] for b in backs])
    theirs = sibling(jnp.stack([b[1] for b in backs]))
    back = jnp.stack([own, theirs], 1).reshape(groups * capacity, width)
    picked = lax.dot_general(selector, back, (((0,), (0,)), ((), ())), preferred_element_type=jnp.float32)
    return (picked * gate_score).astype(jnp.bfloat16)


def plain_program(tokens, route, gate_score, w_gate, w_up, w_down, capacity):
    groups = lax.axis_size("expert")
    target = route[:, 0]
    selector = selector_of(target * capacity + rank_of(target), groups * capacity)
    outgoing = jnp.dot(selector, tokens, preferred_element_type=jnp.float32).astype(jnp.bfloat16)
    arrived = lax.all_to_all(outgoing, "expert", split_axis=0, concat_axis=0, tiled=True)
    whole = lax.all_gather(arrived, "blk", axis=1, tiled=True)
    gate_acc = jnp.dot(whole, w_gate, preferred_element_type=jnp.float32)
    up_acc = jnp.dot(whole, w_up, preferred_element_type=jnp.float32)
    hidden = (jax.nn.silu(gate_acc) * up_acc).astype(jnp.bfloat16)
    partial_sum = jnp.dot(hidden, w_down, preferred_element_type=jnp.float32)
    shares = lax.psum_scatter(partial_sum.astype(jnp.bfloat16), "blk", scatter_dimension=1, tiled=True)
    back = lax.all_to_all(shares, "expert", split_axis=0, concat_axis=0, tiled=True)
    picked = lax.dot_general(selector, back, (((0,), (0,)), ((), ())), preferred_element_type=jnp.float32)
    return (picked * gate_score).astype(jnp.bfloat16)


def per_device(tokens, route, gate_score, w_gate, w_up, w_down):
    groups, n = lax.axis_size("expert"), lax.axis_size("blk")
    count, width = tokens.shape
    capacity = 3 * count // (2 * groups)
    square = n == len(RING) and groups & (groups - 1) == 0 and width % 128 == 0 and capacity % 16 == 0
    program = square_program if square else plain_program
    return program(tokens, route, gate_score, w_gate[0], w_up[0], w_down[0], capacity)


def solution(mesh):
    in_specs = (
        P("expert", "blk"),
        P("expert", None),
        P("expert", None),
        P("expert", None, "blk"),
        P("expert", None, "blk"),
        P("expert", "blk", None),
    )
    return jax.shard_map(
        per_device, mesh=mesh, in_specs=in_specs, out_specs=P("expert", "blk"), check_vma=False
    )
```

time: 247 us -> 152 us (0.62)
  the two profiles are of different devices: /device:TPU:0 before, /device:TPU:17 now
where the time goes in v2:
time: 152 us
  waiting for transfers between devices  83.7 us (55%)
  starting transfers between devices  29.6 us (19%)
  Pallas kernels  24 us (16%)
  local copies, waits for them, and re-layouts  9.47 us (6%)
  matrix products  2.93 us (2%)
  other arithmetic  2.2 us (1%)
    ppermute x6, waiting for transfers between devices, square_program(): lax.ppermute(a, 'expert', [(i, i ^ 2 * k) for i in range(groups)])  53 us
    ppermute x24, waiting for transfers between devices, ring_layer(): step = lambda a: lax.ppermute(a, ('expert', 'blk'), perm)  27.3 us
    ppermute x24, starting transfers between devices, ring_layer(): step = lambda a: lax.ppermute(a, ('expert', 'blk'), perm)  24 us
    pallas_call x4, Pallas kernels, hidden_of(): pl.pallas_call(hidden_kernel, in_specs=[SMEM] + [VMEM] * 7, out_specs=[VM...  12.9 us
    pallas_call x12, Pallas kernels, down_of(): pl.pallas_call(lambda *refs: down_kernel(j, *refs), in_specs=[SMEM] + [VM...  11.1 us
    unnamed x18, local copies, waits for them, and re-layouts  8.39 us
    ppermute x6, starting transfers between devices, square_program(): lax.ppermute(a, 'expert', [(i, i ^ 2 * k) for i in range(groups)])  4.17 us
    ppermute x2, waiting for transfers between devices, square_program(): lax.ppermute(a, 'expert', [(i, i ^ 1) for i in range(groups)])  3.38 us
  transfers between devices with their start and end apart: 32, of which 21 were waited for; matrix products, arithmetic and copies ran while one was open for 1% of the time, Pallas kernels for 16%

profile of v2, /device:TPU:17, one launch (start us, length us, event | category | flops | bytes accessed | tf_op | source)
XLA Modules:
  0.0 152.1 jit_solution(7916733873981406836)
XLA Ops:
  3.6 1.7 %collective-permute-done = bf16[4,96,896]{2,1,0:T(8,128)(2,1)S(1)} collective-permute-done((bf16[4,96,896]{2,1,0:T(8,128)(2,1)S(1)}, bf16[4,96,896]{2,1,0:T(8,128)(2,1)S(1)}, u32[]{:S(2)}, u32[]{:S(2)}) %collective-permute-start) | collective-permute-done | bytes 688160 | tf_op jit(solution)/shard_map/ppermute | solution.py:113
  5.4 1.4 collective-permute-start.7
  6.9 1.3 collective-permute-start.1
  8.3 1.4 collective-permute-start.23
  9.6 10.2 %collective-permute-done.7.x0 = bf16[192,896]{1,0:T(8,128)(2,1)S(1)} collective-permute-done((bf16[192,896]{1,0:T(8,128)(2,1)S(1)}, bf16[192,896]{1,0:T(8,128)(2,1)S(1)}, u32[]{:S(2)}, u32[]{:S(2)}) %collective-permute-start.7) | collective-permute-done | bytes 344096 | tf_op jit(solution)/shard_map/ppermute | solution.py:114
  25.2 12.8 %collective-permute-done.23.x0 = bf16[192,896]{1,0:T(8,128)(2,1)S(1)} collective-permute-done((bf16[192,896]{1,0:T(8,128)(2,1)S(1)}, bf16[192,896]{1,0:T(8,128)(2,1)S(1)}, u32[]{:S(2)}, u32[]{:S(2)}) %collective-permute-start.23) | collective-permute-done | bytes 344096 | tf_op jit(solution)/shard_map/ppermute | solution.py:114
  41.0 3.5 %collective-permute-done.24.x1 = bf16[192,896]{1,0:T(8,128)(2,1)S(1)} collective-permute-done((bf16[192,896]{1,0:T(8,128)(2,1)S(1)}, bf16[192,896]{1,0:T(8,128)(2,1)S(1)}, u32[]{:S(2)}, u32[]{:S(2)}) %collective-permute-start.24) | collective-permute-done | bytes 344096 | tf_op jit(solution)/shard_map/ppermute | solution.py:93
  45.5 2.7 %collective-permute-done.9.x2 = bf16[192,896]{1,0:T(8,128)(2,1)} collective-permute-done((bf16[192,896]{1,0:T(8,128)(2,1)S(1)}, bf16[192,896]{1,0:T(8,128)(2,1)}, u32[]{:S(2)}, u32[]{:S(2)}) %collective-permute-start.9) | collective-permute-done | bytes 344096 | tf_op jit(solution)/shard_map/ppermute | solution.py:93
  49.3 2.6 %collective-permute-done.17.x2 = bf16[192,896]{1,0:T(8,128)(2,1)} collective-permute-done((bf16[192,896]{1,0:T(8,128)(2,1)S(1)}, bf16[192,896]{1,0:T(8,128)(2,1)}, u32[]{:S(2)}, u32[]{:S(2)}) %collective-permute-start.17) | collective-permute-done | bytes 344096 | tf_op jit(solution)/shard_map/ppermute | solution.py:93
  53.7 1.9 %collective-permute-done.3.x3 = bf16[192,896]{1,0:T(8,128)(2,1)} collective-permute-done((bf16[192,896]{1,0:T(8,128)(2,1)}, bf16[192,896]{1,0:T(8,128)(2,1)}, u32[]{:S(2)}, u32[]{:S(2)}) %collective-permute-start.3) | collective-permute-done | bytes 344096 | tf_op jit(solution)/shard_map/ppermute | solution.py:93
  55.6 2.0 %copy-done.1 = bf16[1,512,3584]{2,1,0:T(8,128)(2,1)S(1)} copy-done((bf16[1,512,3584]{2,1,0:T(8,128)(2,1)S(1)}, bf16[1,512,3584]{2,1,0:T(8,128)(2,1)}, u32[]{:S(2)}) %copy-start.1) | copy-done | bytes 3670040
  57.6 2.0 %copy-done.3 = bf16[1,3584,512]{2,1,0:T(8,128)(2,1)S(1)} copy-done((bf16[1,3584,512]{2,1,0:T(8,128)(2,1)S(1)}, bf16[1,3584,512]{2,1,0:T(8,128)(2,1)}, u32[]{:S(2)}) %copy-start.3) | copy-done | bytes 3670040
  59.7 2.0 %copy-done.5 = bf16[1,3584,512]{2,1,0:T(8,128)(2,1)S(1)} copy-done((bf16[1,3584,512]{2,1,0:T(8,128)(2,1)S(1)}, bf16[1,3584,512]{2,1,0:T(8,128)(2,1)}, u32[]{:S(2)}) %copy-start.5) | copy-done | bytes 3670040
  62.7 3.2 %shard_map.73 = (bf16[192,512]{1,0:T(8,128)(2,1)S(1)}, bf16[192,896]{1,0:T(8,128)(2,1)S(1)}) custom-call(s32[4]{0:T(128)S(1)} %dynamic-slice_bitcast_fusion.order.refs_0_, bf16[192,896]{1,0:T(8,128)(2,1)S(1)} %pad_maximum_fusion.2.x0, bf16[192,896]{1,0:T(8,128)(2,1)S(1)} %copy-done.7, bf16[192,896]{1,0:T(8,128)(2,1)} %collective-permute-done.2.x2, ...), custom_call_target="tpu_custom_call" | custom-call | flops 1585446912 | bytes 11010048 | tf_op jit(solution)/shard_map/pallas_call | solution.py:53
  68.3 3.3 %shard_map.77 = (bf16[192,512]{1,0:T(8,128)(2,1)S(1)}, bf16[192,896]{1,0:T(8,128)(2,1)S(1)}) custom-call(s32[4]{0:T(128)S(1)} %dynamic-slice_bitcast_fusion.order.refs_0_, bf16[192,896]{1,0:T(8,128)(2,1)S(1)} %collective-permute-done.7.x0, bf16[192,896]{1,0:T(8,128)(2,1)S(1)} %collective-permute-done.8.x1, bf16[192,896]{1,0:T(8,128)(2,1)} %collective-permute-done.9.x2, ...), custom_call_target="tpu_custom_call" | custom-call | flops 1585446912 | bytes 11010048 | tf_op jit(solution)/shard_map/pallas_call | solution.py:53
  71.9 3.3 %shard_map.81 = (bf16[192,512]{1,0:T(8,128)(2,1)S(1)}, bf16[192,896]{1,0:T(8,128)(2,1)S(1)}) custom-call(s32[4]{0:T(128)S(1)} %dynamic-slice_bitcast_fusion.order.refs_0_, bf16[192,896]{1,0:T(8,128)(2,1)S(1)} %collective-permute-done.15.x0, bf16[192,896]{1,0:T(8,128)(2,1)S(1)} %collective-permute-done.16.x1, bf16[192,896]{1,0:T(8,128)(2,1)} %collective-permute-done.17.x2, ...), custom_call_target="tpu_custom_call" | custom-call | flops 1585446912 | bytes 11010048 | tf_op jit(solution)/shard_map/pallas_call | solution.py:53
  76.1 3.1 %shard_map.85 = (bf16[192,512]{1,0:T(8,128)(2,1)S(1)}, bf16[192,896]{1,0:T(8,128)(2,1)S(1)}) custom-call(s32[4]{0:T(128)S(1)} %dynamic-slice_bitcast_fusion.order.refs_0_, bf16[192,896]{1,0:T(8,128)(2,1)S(1)} %collective-permute-done.23.x0, bf16[192,896]{1,0:T(8,128)(2,1)S(1)} %collective-permute-done.24.x1, bf16[192,896]{1,0:T(8,128)(2,1)} %collective-permute-done.25.x2, ...), custom_call_target="tpu_custom_call" | custom-call | flops 1585446912 | bytes 11010048 | tf_op jit(solution)/shard_map/pallas_call | solution.py:53
  81.3 1.2 collective-permute-start.12
  85.5 1.6 %collective-permute-done.27.refs_2_ = bf16[192,896]{1,0:T(8,128)(2,1)S(1)} collective-permute-done((bf16[192,896]{1,0:T(8,128)(2,1)S(1)}, bf16[192,896]{1,0:T(8,128)(2,1)S(1)}, u32[]{:S(2)}, u32[]{:S(2)}) %collective-permute-start.27) | collective-permute-done | bytes 344096 | tf_op jit(solution)/shard_map/ppermute | solution.py:93
  89.2 1.6 %collective-permute-done.12.refs_2_ = bf16[192,896]{1,0:T(8,128)(2,1)S(1)} collective-permute-done((bf16[192,896]{1,0:T(8,128)(2,1)S(1)}, bf16[192,896]{1,0:T(8,128)(2,1)S(1)}, u32[]{:S(2)}, u32[]{:S(2)}) %collective-permute-start.12) | collective-permute-done | bytes 344096 | tf_op jit(solution)/shard_map/ppermute | solution.py:93
  92.9 1.6 %collective-permute-done.5.refs_2_ = bf16[192,896]{1,0:T(8,128)(2,1)S(1)} collective-permute-done((bf16[192,896]{1,0:T(8,128)(2,1)S(1)}, bf16[192,896]{1,0:T(8,128)(2,1)S(1)}, u32[]{:S(2)}, u32[]{:S(2)}) %collective-permute-start.5) | collective-permute-done | bytes 344096 | tf_op jit(solution)/shard_map/ppermute | solution.py:93
  95.4 1.4 collective-permute-start.6
  96.8 1.4 collective-permute-done.20.refs_2_
  100.3 1.6 %collective-permute-done.28.refs_2_ = bf16[192,896]{1,0:T(8,128)(2,1)S(1)} collective-permute-done((bf16[192,896]{1,0:T(8,128)(2,1)S(1)}, bf16[192,896]{1,0:T(8,128)(2,1)S(1)}, u32[]{:S(2)}, u32[]{:S(2)}) %collective-permute-start.28) | collective-permute-done | bytes 344096 | tf_op jit(solution)/shard_map/ppermute | solution.py:93
  104.0 1.6 %collective-permute-done.13.refs_2_ = bf16[192,896]{1,0:T(8,128)(2,1)S(1)} collective-permute-done((bf16[192,896]{1,0:T(8,128)(2,1)S(1)}, bf16[192,896]{1,0:T(8,128)(2,1)S(1)}, u32[]{:S(2)}, u32[]{:S(2)}) %collective-permute-start.13) | collective-permute-done | bytes 344096 | tf_op jit(solution)/shard_map/ppermute | solution.py:93
  107.6 1.6 %collective-permute-done.6.refs_2_ = bf16[192,896]{1,0:T(8,128)(2,1)S(1)} collective-permute-done((bf16[192,896]{1,0:T(8,128)(2,1)S(1)}, bf16[192,896]{1,0:T(8,128)(2,1)S(1)}, u32[]{:S(2)}, u32[]{:S(2)}) %collective-permute-start.6) | collective-permute-done | bytes 344096 | tf_op jit(solution)/shard_map/ppermute | solution.py:93
  110.2 2.8 %collective-permute-done.21.refs_2_ = bf16[192,896]{1,0:T(8,128)(2,1)S(1)} collective-permute-done((bf16[192,896]{1,0:T(8,128)(2,1)S(1)}, bf16[192,896]{1,0:T(8,128)(2,1)S(1)}, u32[]{:S(2)}, u32[]{:S(2)}) %collective-permute-start.21) | collective-permute-done | bytes 344096 | tf_op jit(solution)/shard_map/ppermute | solution.py:93
  114.0 2.6 %collective-permute-done.29.refs_2_ = bf16[192,896]{1,0:T(8,128)(2,1)S(1)} collective-permute-done((bf16[192,896]{1,0:T(8,128)(2,1)S(1)}, bf16[192,896]{1,0:T(8,128)(2,1)S(1)}, u32[]{:S(2)}, u32[]{:S(2)}) %collective-permute-start.29) | collective-permute-done | bytes 344096 | tf_op jit(solution)/shard_map/ppermute | solution.py:93
  117.7 17.2 %collective-permute-done.22 = bf16[192,896]{1,0:T(8,128)(2,1)S(1)} collective-permute-done((bf16[192,896]{1,0:T(8,128)(2,1)S(1)}, bf16[192,896]{1,0:T(8,128)(2,1)S(1)}, u32[]{:S(2)}, u32[]{:S(2)}) %collective-permute-start.22) | collective-permute-done | bytes 344096 | tf_op jit(solution)/shard_map/ppermute | solution.py:114
  135.0 11.8 %collective-permute-done.30 = bf16[192,896]{1,0:T(8,128)(2,1)S(1)} collective-permute-done((bf16[192,896]{1,0:T(8,128)(2,1)S(1)}, bf16[192,896]{1,0:T(8,128)(2,1)S(1)}, u32[]{:S(2)}, u32[]{:S(2)}) %collective-permute-start.30) | collective-permute-done | bytes 344096 | tf_op jit(solution)/shard_map/ppermute | solution.py:114
  147.6 1.7 %collective-permute-done.31 = bf16[4,96,896]{2,1,0:T(8,128)(2,1)S(1)} collective-permute-done((bf16[4,96,896]{2,1,0:T(8,128)(2,1)S(1)}, bf16[4,96,896]{2,1,0:T(8,128)(2,1)S(1)}, u32[]{:S(2)}, u32[]{:S(2)}) %collective-permute-start.31) | collective-permute-done | bytes 688160 | tf_op jit(solution)/shard_map/ppermute | solution.py:113
  150.1 2.0 %multiply_convert_fusion = bf16[512,896]{1,0:T(8,128)(2,1)} fusion(bf16[768,896]{1,0:T(8,128)(2,1)S(1)} %bitcast.74, f32[512]{0:T(512)S(1)} %bitcast.78, s32[512]{0:T(512)S(1)} %multiply_add_fusion), kind=kOutput, calls=%fused_computation | convolution fusion | flops 705953792 | bytes 2297856 | tf_op jit(solution)/shard_map/dot_general | solution.py:129
  (86 shorter events, 42.0 us)
Async XLA Ops:
  2.8 2.5 %collective-permute-start = (bf16[4,96,896]{2,1,0:T(8,128)(2,1)S(1)}, bf16[4,96,896]{2,1,0:T(8,128)(2,1)S(1)}, u32[]{:S(2)}, u32[]{:S(2)}) collective-permute-start(bf16[4,96,896]{2,1,0:T(8,128)(2,1)S(1)} %slice_bitcast_fusion), channel_id=1, source_target_pairs={{0,4},{4,0},{8,12},{12,8},{16,20},{20,16},{24,28},{28,24},{1,5},{5... | collective-permute-start | bytes 2064392 | tf_op jit(solution)/shard_map/ppermute | solution.py:113
  5.4 14.5 %collective-permute-start.7 = (bf16[192,896]{1,0:T(8,128)(2,1)S(1)}, bf16[192,896]{1,0:T(8,128)(2,1)S(1)}, u32[]{:S(2)}, u32[]{:S(2)}) collective-permute-start(bf16[192,896]{1,0:T(8,128)(2,1)S(1)} %pad_maximum_fusion.3), channel_id=1, source_target_pairs={{0,8},{4,12},{8,0},{12,4},{16,24},{20,28},{24,16},{28,20},{1,9},{5... | collective-permute-start | bytes 1032200 | tf_op jit(solution)/shard_map/ppermute | solution.py:114
  6.8 15.3 %collective-permute-start.15 = (bf16[192,896]{1,0:T(8,128)(2,1)S(1)}, bf16[192,896]{1,0:T(8,128)(2,1)S(1)}, u32[]{:S(2)}, u32[]{:S(2)}) collective-permute-start(bf16[192,896]{1,0:T(8,128)(2,1)S(1)} %pad_maximum_fusion.4), channel_id=1, source_target_pairs={{0,16},{4,20},{8,24},{12,28},{16,0},{20,4},{24,8},{28,12},{1,17},{... | collective-permute-start | bytes 1032200 | tf_op jit(solution)/shard_map/ppermute | solution.py:114
  6.9 16.3 %collective-permute-start.1 = (bf16[192,896]{1,0:T(8,128)(2,1)S(1)}, bf16[192,896]{1,0:T(8,128)(2,1)S(1)}, u32[]{:S(2)}, u32[]{:S(2)}) collective-permute-start(bf16[192,896]{1,0:T(8,128)(2,1)S(1)} %pad_maximum_fusion.2.x0), channel_id=1, source_target_pairs={{0,1},{1,3},{3,2},{2,0},{4,6},{5,4},{7,5},{6,7},{8,9},{9,11},{11,1... | collective-permute-start | bytes 1032200 | tf_op jit(solution)/shard_map/ppermute | solution.py:93
  8.3 29.7 %collective-permute-start.23 = (bf16[192,896]{1,0:T(8,128)(2,1)S(1)}, bf16[192,896]{1,0:T(8,128)(2,1)S(1)}, u32[]{:S(2)}, u32[]{:S(2)}) collective-permute-start(bf16[192,896]{1,0:T(8,128)(2,1)S(1)} %pad_maximum_fusion.5), channel_id=1, source_target_pairs={{0,24},{4,28},{8,16},{12,20},{16,8},{20,12},{24,0},{28,4},{1,25},{... | collective-permute-start | bytes 1032200 | tf_op jit(solution)/shard_map/ppermute | solution.py:114
  19.9 19.3 %collective-permute-start.8 = (bf16[192,896]{1,0:T(8,128)(2,1)S(1)}, bf16[192,896]{1,0:T(8,128)(2,1)S(1)}, u32[]{:S(2)}, u32[]{:S(2)}) collective-permute-start(bf16[192,896]{1,0:T(8,128)(2,1)S(1)} %collective-permute-done.7.x0), channel_id=1, source_target_pairs={{0,1},{1,3},{3,2},{2,0},{4,6},{5,4},{7,5},{6,7},{8,9},{9,11},{11,1... | collective-permute-start | bytes 1032200 | tf_op jit(solution)/shard_map/ppermute | solution.py:93
  22.0 18.3 %collective-permute-start.16 = (bf16[192,896]{1,0:T(8,128)(2,1)S(1)}, bf16[192,896]{1,0:T(8,128)(2,1)S(1)}, u32[]{:S(2)}, u32[]{:S(2)}) collective-permute-start(bf16[192,896]{1,0:T(8,128)(2,1)S(1)} %collective-permute-done.15.x0), channel_id=1, source_target_pairs={{0,1},{1,3},{3,2},{2,0},{4,6},{5,4},{7,5},{6,7},{8,9},{9,11},{11,1... | collective-permute-start | bytes 1032200 | tf_op jit(solution)/shard_map/ppermute | solution.py:93
  23.3 17.3 %collective-permute-start.2 = (bf16[192,896]{1,0:T(8,128)(2,1)S(1)}, bf16[192,896]{1,0:T(8,128)(2,1)}, u32[]{:S(2)}, u32[]{:S(2)}) collective-permute-start(bf16[192,896]{1,0:T(8,128)(2,1)S(1)} %collective-permute-done.1.x1), channel_id=1, source_target_pairs={{0,1},{1,3},{3,2},{2,0},{4,6},{5,4},{7,5},{6,7},{8,9},{9,11},{11,1... | collective-permute-start | bytes 1032200 | tf_op jit(solution)/shard_map/ppermute | solution.py:93
  38.0 6.4 %collective-permute-start.24 = (bf16[192,896]{1,0:T(8,128)(2,1)S(1)}, bf16[192,896]{1,0:T(8,128)(2,1)S(1)}, u32[]{:S(2)}, u32[]{:S(2)}) collective-permute-start(bf16[192,896]{1,0:T(8,128)(2,1)S(1)} %collective-permute-done.23.x0), channel_id=1, source_target_pairs={{0,1},{1,3},{3,2},{2,0},{4,6},{5,4},{7,5},{6,7},{8,9},{9,11},{11,1... | collective-permute-start | bytes 1032200 | tf_op jit(solution)/shard_map/ppermute | solution.py:93
  39.2 9.1 %collective-permute-start.9 = (bf16[192,896]{1,0:T(8,128)(2,1)S(1)}, bf16[192,896]{1,0:T(8,128)(2,1)}, u32[]{:S(2)}, u32[]{:S(2)}) collective-permute-start(bf16[192,896]{1,0:T(8,128)(2,1)S(1)} %collective-permute-done.8.x1), channel_id=1, source_target_pairs={{0,1},{1,3},{3,2},{2,0},{4,6},{5,4},{7,5},{6,7},{8,9},{9,11},{11,1... | collective-permute-start | bytes 1032200 | tf_op jit(solution)/shard_map/ppermute | solution.py:93
  40.4 11.5 %collective-permute-start.17 = (bf16[192,896]{1,0:T(8,128)(2,1)S(1)}, bf16[192,896]{1,0:T(8,128)(2,1)}, u32[]{:S(2)}, u32[]{:S(2)}) collective-permute-start(bf16[192,896]{1,0:T(8,128)(2,1)S(1)} %collective-permute-done.16.x1), channel_id=1, source_target_pairs={{0,1},{1,3},{3,2},{2,0},{4,6},{5,4},{7,5},{6,7},{8,9},{9,11},{11,1... | collective-permute-start | bytes 1032200 | tf_op jit(solution)/shard_map/ppermute | solution.py:93
  40.6 15.0 %collective-permute-start.3 = (bf16[192,896]{1,0:T(8,128)(2,1)}, bf16[192,896]{1,0:T(8,128)(2,1)}, u32[]{:S(2)}, u32[]{:S(2)}) collective-permute-start(bf16[192,896]{1,0:T(8,128)(2,1)} %collective-permute-done.2.x2), channel_id=1, source_target_pairs={{0,1},{1,3},{3,2},{2,0},{4,6},{5,4},{7,5},{6,7},{8,9},{9,11},{11,1... | collective-permute-start | bytes 1032200 | tf_op jit(solution)/shard_map/ppermute | solution.py:93
  44.4 22.7 %collective-permute-start.25 = (bf16[192,896]{1,0:T(8,128)(2,1)S(1)}, bf16[192,896]{1,0:T(8,128)(2,1)}, u32[]{:S(2)}, u32[]{:S(2)}) collective-permute-start(bf16[192,896]{1,0:T(8,128)(2,1)S(1)} %collective-permute-done.24.x1), channel_id=1, source_target_pairs={{0,1},{1,3},{3,2},{2,0},{4,6},{5,4},{7,5},{6,7},{8,9},{9,11},{11,1... | collective-permute-start | bytes 1032200 | tf_op jit(solution)/shard_map/ppermute | solution.py:93
  48.2 20.1 %collective-permute-start.10 = (bf16[192,896]{1,0:T(8,128)(2,1)}, bf16[192,896]{1,0:T(8,128)(2,1)}, u32[]{:S(2)}, u32[]{:S(2)}) collective-permute-start(bf16[192,896]{1,0:T(8,128)(2,1)} %collective-permute-done.9.x2), channel_id=1, source_target_pairs={{0,1},{1,3},{3,2},{2,0},{4,6},{5,4},{7,5},{6,7},{8,9},{9,11},{11,1... | collective-permute-start | bytes 1032200 | tf_op jit(solution)/shard_map/ppermute | solution.py:93
  51.9 20.0 %collective-permute-start.18 = (bf16[192,896]{1,0:T(8,128)(2,1)}, bf16[192,896]{1,0:T(8,128)(2,1)S(1)}, u32[]{:S(2)}, u32[]{:S(2)}) collective-permute-start(bf16[192,896]{1,0:T(8,128)(2,1)} %collective-permute-done.17.x2), channel_id=1, source_target_pairs={{0,1},{1,3},{3,2},{2,0},{4,6},{5,4},{7,5},{6,7},{8,9},{9,11},{11,1... | collective-permute-start | bytes 1032200 | tf_op jit(solution)/shard_map/ppermute | solution.py:93
  65.9 16.7 %collective-permute-start.4 = (bf16[192,896]{1,0:T(8,128)(2,1)S(1)}, bf16[192,896]{1,0:T(8,128)(2,1)S(1)}, u32[]{:S(2)}, u32[]{:S(2)}) collective-permute-start(bf16[192,896]{1,0:T(8,128)(2,1)S(1)} %get-tuple-element.14), channel_id=1, source_target_pairs={{0,1},{1,3},{3,2},{2,0},{4,6},{5,4},{7,5},{6,7},{8,9},{9,11},{11,1... | collective-permute-start | bytes 1032200 | tf_op jit(solution)/shard_map/ppermute | solution.py:93
  67.1 9.0 %collective-permute-start.26 = (bf16[192,896]{1,0:T(8,128)(2,1)}, bf16[192,896]{1,0:T(8,128)(2,1)S(1)}, u32[]{:S(2)}, u32[]{:S(2)}) collective-permute-start(bf16[192,896]{1,0:T(8,128)(2,1)} %collective-permute-done.25.x2), channel_id=1, source_target_pairs={{0,1},{1,3},{3,2},{2,0},{4,6},{5,4},{7,5},{6,7},{8,9},{9,11},{11,1... | collective-permute-start | bytes 1032200 | tf_op jit(solution)/shard_map/ppermute | solution.py:93
  71.6 8.8 %collective-permute-start.11 = (bf16[192,896]{1,0:T(8,128)(2,1)S(1)}, bf16[192,896]{1,0:T(8,128)(2,1)S(1)}, u32[]{:S(2)}, u32[]{:S(2)}) collective-permute-start(bf16[192,896]{1,0:T(8,128)(2,1)S(1)} %get-tuple-element.16), channel_id=1, source_target_pairs={{0,1},{1,3},{3,2},{2,0},{4,6},{5,4},{7,5},{6,7},{8,9},{9,11},{11,1... | collective-permute-start | bytes 1032200 | tf_op jit(solution)/shard_map/ppermute | solution.py:93
  75.2 8.9 %collective-permute-start.19 = (bf16[192,896]{1,0:T(8,128)(2,1)S(1)}, bf16[192,896]{1,0:T(8,128)(2,1)S(1)}, u32[]{:S(2)}, u32[]{:S(2)}) collective-permute-start(bf16[192,896]{1,0:T(8,128)(2,1)S(1)} %get-tuple-element.18), channel_id=1, source_target_pairs={{0,1},{1,3},{3,2},{2,0},{4,6},{5,4},{7,5},{6,7},{8,9},{9,11},{11,1... | collective-permute-start | bytes 1032200 | tf_op jit(solution)/shard_map/ppermute | solution.py:93
  79.2 7.9 %collective-permute-start.27 = (bf16[192,896]{1,0:T(8,128)(2,1)S(1)}, bf16[192,896]{1,0:T(8,128)(2,1)S(1)}, u32[]{:S(2)}, u32[]{:S(2)}) collective-permute-start(bf16[192,896]{1,0:T(8,128)(2,1)S(1)} %get-tuple-element.20), channel_id=1, source_target_pairs={{0,1},{1,3},{3,2},{2,0},{4,6},{5,4},{7,5},{6,7},{8,9},{9,11},{11,1... | collective-permute-start | bytes 1032200 | tf_op jit(solution)/shard_map/ppermute | solution.py:93
  81.3 9.5 %collective-permute-start.12 = (bf16[192,896]{1,0:T(8,128)(2,1)S(1)}, bf16[192,896]{1,0:T(8,128)(2,1)S(1)}, u32[]{:S(2)}, u32[]{:S(2)}) collective-permute-start(bf16[192,896]{1,0:T(8,128)(2,1)S(1)} %shard_map.78), channel_id=1, source_target_pairs={{0,1},{1,3},{3,2},{2,0},{4,6},{5,4},{7,5},{6,7},{8,9},{9,11},{11,1... | collective-permute-start | bytes 1032200 | tf_op jit(solution)/shard_map/ppermute | solution.py:93
  83.5 11.0 %collective-permute-start.5 = (bf16[192,896]{1,0:T(8,128)(2,1)S(1)}, bf16[192,896]{1,0:T(8,128)(2,1)S(1)}, u32[]{:S(2)}, u32[]{:S(2)}) collective-permute-start(bf16[192,896]{1,0:T(8,128)(2,1)S(1)} %shard_map.74), channel_id=1, source_target_pairs={{0,1},{1,3},{3,2},{2,0},{4,6},{5,4},{7,5},{6,7},{8,9},{9,11},{11,1... | collective-permute-start | bytes 1032200 | tf_op jit(solution)/shard_map/ppermute | solution.py:93
  85.0 13.2 %collective-permute-start.20 = (bf16[192,896]{1,0:T(8,128)(2,1)S(1)}, bf16[192,896]{1,0:T(8,128)(2,1)S(1)}, u32[]{:S(2)}, u32[]{:S(2)}) collective-permute-start(bf16[192,896]{1,0:T(8,128)(2,1)S(1)} %shard_map.82), channel_id=1, source_target_pairs={{0,1},{1,3},{3,2},{2,0},{4,6},{5,4},{7,5},{6,7},{8,9},{9,11},{11,1... | collective-permute-start | bytes 1032200 | tf_op jit(solution)/shard_map/ppermute | solution.py:93
  88.0 13.8 %collective-permute-start.28 = (bf16[192,896]{1,0:T(8,128)(2,1)S(1)}, bf16[192,896]{1,0:T(8,128)(2,1)S(1)}, u32[]{:S(2)}, u32[]{:S(2)}) collective-permute-start(bf16[192,896]{1,0:T(8,128)(2,1)S(1)} %shard_map.86), channel_id=1, source_target_pairs={{0,1},{1,3},{3,2},{2,0},{4,6},{5,4},{7,5},{6,7},{8,9},{9,11},{11,1... | collective-permute-start | bytes 1032200 | tf_op jit(solution)/shard_map/ppermute | solution.py:93
  91.7 13.8 %collective-permute-start.13 = (bf16[192,896]{1,0:T(8,128)(2,1)S(1)}, bf16[192,896]{1,0:T(8,128)(2,1)S(1)}, u32[]{:S(2)}, u32[]{:S(2)}) collective-permute-start(bf16[192,896]{1,0:T(8,128)(2,1)S(1)} %shard_map.79), channel_id=1, source_target_pairs={{0,1},{1,3},{3,2},{2,0},{4,6},{5,4},{7,5},{6,7},{8,9},{9,11},{11,1... | collective-permute-start | bytes 1032200 | tf_op jit(solution)/shard_map/ppermute | solution.py:93
  95.4 13.8 %collective-permute-start.6 = (bf16[192,896]{1,0:T(8,128)(2,1)S(1)}, bf16[192,896]{1,0:T(8,128)(2,1)S(1)}, u32[]{:S(2)}, u32[]{:S(2)}) collective-permute-start(bf16[192,896]{1,0:T(8,128)(2,1)S(1)} %shard_map.75), channel_id=1, source_target_pairs={{0,1},{1,3},{3,2},{2,0},{4,6},{5,4},{7,5},{6,7},{8,9},{9,11},{11,1... | collective-permute-start | bytes 1032200 | tf_op jit(solution)/shard_map/ppermute | solution.py:93
  99.1 13.8 %collective-permute-start.21 = (bf16[192,896]{1,0:T(8,128)(2,1)S(1)}, bf16[192,896]{1,0:T(8,128)(2,1)S(1)}, u32[]{:S(2)}, u32[]{:S(2)}) collective-permute-start(bf16[192,896]{1,0:T(8,128)(2,1)S(1)} %shard_map.83), channel_id=1, source_target_pairs={{0,1},{1,3},{3,2},{2,0},{4,6},{5,4},{7,5},{6,7},{8,9},{9,11},{11,1... | collective-permute-start | bytes 1032200 | tf_op jit(solution)/shard_map/ppermute | solution.py:93
  102.8 13.8 %collective-permute-start.29 = (bf16[192,896]{1,0:T(8,128)(2,1)S(1)}, bf16[192,896]{1,0:T(8,128)(2,1)S(1)}, u32[]{:S(2)}, u32[]{:S(2)}) collective-permute-start(bf16[192,896]{1,0:T(8,128)(2,1)S(1)} %shard_map.87), channel_id=1, source_target_pairs={{0,1},{1,3},{3,2},{2,0},{4,6},{5,4},{7,5},{6,7},{8,9},{9,11},{11,1... | collective-permute-start | bytes 1032200 | tf_op jit(solution)/shard_map/ppermute | solution.py:93
  106.5 11.2 %collective-permute-start.14 = (bf16[192,896]{1,0:T(8,128)(2,1)S(1)}, bf16[192,896]{1,0:T(8,128)(2,1)S(1)}, u32[]{:S(2)}, u32[]{:S(2)}) collective-permute-start(bf16[192,896]{1,0:T(8,128)(2,1)S(1)} %shard_map.80), channel_id=1, source_target_pairs={{0,8},{4,12},{8,0},{12,4},{16,24},{20,28},{24,16},{28,20},{1,9},{5... | collective-permute-start | bytes 1032200 | tf_op jit(solution)/shard_map/ppermute | solution.py:114
  113.8 21.1 %collective-permute-start.22 = (bf16[192,896]{1,0:T(8,128)(2,1)S(1)}, bf16[192,896]{1,0:T(8,128)(2,1)S(1)}, u32[]{:S(2)}, u32[]{:S(2)}) collective-permute-start(bf16[192,896]{1,0:T(8,128)(2,1)S(1)} %shard_map.84), channel_id=1, source_target_pairs={{0,16},{4,20},{8,24},{12,28},{16,0},{20,4},{24,8},{28,12},{1,17},{... | collective-permute-start | bytes 1032200 | tf_op jit(solution)/shard_map/ppermute | solution.py:114
  117.5 29.2 %collective-permute-start.30 = (bf16[192,896]{1,0:T(8,128)(2,1)S(1)}, bf16[192,896]{1,0:T(8,128)(2,1)S(1)}, u32[]{:S(2)}, u32[]{:S(2)}) collective-permute-start(bf16[192,896]{1,0:T(8,128)(2,1)S(1)} %shard_map.88), channel_id=1, source_target_pairs={{0,24},{4,28},{8,16},{12,20},{16,8},{20,12},{24,0},{28,4},{1,25},{... | collective-permute-start | bytes 1032200 | tf_op jit(solution)/shard_map/ppermute | solution.py:114
  146.9 2.4 %collective-permute-start.31 = (bf16[4,96,896]{2,1,0:T(8,128)(2,1)S(1)}, bf16[4,96,896]{2,1,0:T(8,128)(2,1)S(1)}, u32[]{:S(2)}, u32[]{:S(2)}) collective-permute-start(bf16[4,96,896]{2,1,0:T(8,128)(2,1)S(1)} %pad_maximum_fusion.1), channel_id=1, source_target_pairs={{0,4},{4,0},{8,12},{12,8},{16,20},{20,16},{24,28},{28,24},{1,5},{5... | collective-permute-start | bytes 2064392 | tf_op jit(solution)/shard_map/ppermute | solution.py:113
  (9 other events, 18.7 us)

commit v3 on v2

--- a/solution.py
+++ b/solution.py
@@ -43,7 +43,24 @@
 
 SMEM = pl.BlockSpec(memory_space=pltpu.SMEM)
 VMEM = pl.BlockSpec(memory_space=pltpu.VMEM)
-LIMIT = pltpu.CompilerParams(vmem_limit_bytes=32 * 1024 * 1024)
+COST = pl.CostEstimate(flops=1, bytes_accessed=1, transcendentals=0)
+LIMIT = pltpu.CompilerParams(vmem_limit_bytes=12 * 1024 * 1024)
+
+
+def order_kernel(order, wg, wu, wd, out):
+    for j in range(order.shape[0]):
+        out[j] = order[j]
+
+
+def order_of(order, wg, wu, wd):
+    return pl.pallas_call(
+        order_kernel,
+        in_specs=[SMEM] + [VMEM] * 3,
+        out_specs=SMEM,
+        out_shape=jax.ShapeDtypeStruct(order.shape, order.dtype),
+        compiler_params=LIMIT,
+        cost_estimate=COST,
+    )(order, wg, wu, wd)
 
 
 def hidden_of(order, xs, wg, wu, wd):
@@ -59,9 +76,7 @@
             jax.ShapeDtypeStruct((rows, width), jnp.bfloat16),
         ],
         compiler_params=LIMIT,
-        cost_estimate=pl.CostEstimate(
-            flops=2 * rows * width * hid * (2 * n + 1), bytes_accessed=6 * n * width * hid, transcendentals=rows * hid
-        ),
+        cost_estimate=COST,
     )(order, *xs, wg, wu, wd)
 
 
@@ -74,9 +89,7 @@
         out_specs=VMEM,
         out_shape=jax.ShapeDtypeStruct((rows, width), jnp.bfloat16),
         compiler_params=LIMIT,
-        cost_estimate=pl.CostEstimate(
-            flops=2 * rows * width * hid, bytes_accessed=2 * width * hid + 4 * rows * width, transcendentals=0
-        ),
+        cost_estimate=COST,
     )(order, hidden, arrived, wd)
 
 
@@ -89,15 +102,15 @@
     return pairs
 
 
-def ring_layer(held, order, perm, wg, wu, wd):
-    step = lambda a: lax.ppermute(a, ("expert", "blk"), perm)
-    xs = [held]
-    for _ in range(3):
-        xs.append(step(xs[-1]))
-    hidden, part = hidden_of(order, xs, wg, wu, wd)
-    for j in (2, 3, 0):
-        part = down_of(j, order, hidden, step(part), wd)
-    return part
+def after(value, *done):
+    return lax.optimization_barrier((value, *done))[0]
+
+
+def turns_of(chunks):
+    return TURNS if chunks == 4 else [k for _ in range(9) for k in range(chunks)]
+
+
+TURNS = (1, 0, 1, 2, 0, 1, 2, 2, 1, 3, 2, 0, 1, 3, 2, 3, 2, 3, 2, 3, 1, 3, 2, 1, 3, 0, 0, 0, 3, 1, 2, 1, 0, 3)
 
 
 def square_program(tokens, route, gate_score, wg, wu, wd, capacity):
@@ -111,21 +124,59 @@
     chunks, width = groups // 2, tokens.shape[1]
     outgoing = outgoing.reshape(chunks, 2, capacity, width)
     sibling = lambda a: lax.ppermute(a, "expert", [(i, i ^ 1) for i in range(groups)])
-    other = lambda a, k: lax.ppermute(a, "expert", [(i, i ^ (2 * k)) for i in range(groups)]) if k else a
-    swapped = sibling(outgoing[:, 1])
+    other = lambda a, k: lax.ppermute(a, "expert", [(i, i ^ (2 * k)) for i in range(groups)])
     perm = ring_perm(groups, n)
+    step = lambda a: lax.ppermute(a, ("expert", "blk"), perm)
     forward = {RING[i]: [RING[(i - s) % n] for s in range(n)] for i in range(n)}
     backward = {RING[i]: [RING[(i + s) % n] for s in range(n)] for i in range(n)}
     table = jnp.array([[forward[i] for i in range(n)], [backward[i] for i in range(n)]], jnp.int32)
     order = table[me % 2, place]
-    backs = [None] * chunks
+
+    swapped = sibling(outgoing[:, 1])
+    packed = [jnp.concatenate([outgoing[k, 0], swapped[k]], 0) for k in range(chunks)]
+    last = [order]
+    pieces = {}
+
+    def event(value):
+        last[0] = after(value, last[0])
+        return last[0]
+
+    def chunk(k):
+        held = packed[k]
+        if k:
+            held = other(held, k)
+            yield
+            held = event(held)
+        xs = [held]
+        for _ in range(n - 1):
+            held = step(held)
+            yield
+            held = event(held)
+            xs.append(held)
+        hidden, part = hidden_of(order, xs, wg, wu, wd)
+        for j in (*range(2, n), 0):
+            part = step(part)
+            yield
+            part = down_of(j, order, hidden, event(part), wd)
+            last[0] = part
+        if k:
+            part = other(part, k)
+            yield
+            part = event(part)
+        theirs = sibling(part[capacity:])
+        yield
+        pieces[k] = [part[:capacity], event(theirs)]
+
+    ways = [chunk(k) for k in range(chunks)]
     for k in range(chunks):
-        chunk = jnp.concatenate([outgoing[k, 0], swapped[k]], 0)
-        shares = ring_layer(other(chunk, k), order, perm, wg, wu, wd)
-        backs[k] = other(shares, k).reshape(2, capacity, width)
-    own = jnp.stack([b[0] for b in backs])
-    theirs = sibling(jnp.stack([b[1] for b in backs]))
-    back = jnp.stack([own, theirs], 1).reshape(groups * capacity, width)
+        next(ways[k])
+    for turn, k in enumerate(turns_of(chunks)):
+        with jax.named_scope("chunk%d" % k):
+            next(ways[k], None)
+        if turn == 1:
+            order = last[0] = order_of(after(order, last[0]), wg, wu, wd)
+    assert len(pieces) == chunks
+    back = jnp.concatenate([piece for k in range(chunks) for piece in pieces[k]], 0)
     picked = lax.dot_general(selector, back, (((0,), (0,)), ((), ())), preferred_element_type=jnp.float32)
     return (picked * gate_score).astype(jnp.bfloat16)
 

time: 152 us -> 143 us (0.941)
  the two profiles are of different devices: /device:TPU:17 before, /device:TPU:0 now
where the time goes in v3:
time: 143 us
  waiting for transfers between devices  71.1 us (50%)
  starting transfers between devices  36.8 us (26%)
  Pallas kernels  22.9 us (16%)
  local copies, waits for them, and re-layouts  7.22 us (5%)
  matrix products  2.94 us (2%)
  other arithmetic  1.86 us (1%)
    ppermute x24, waiting for transfers between devices, square_program(): step = lambda a: lax.ppermute(a, ('expert', 'blk'), perm)  48.2 us
    ppermute x24, starting transfers between devices, square_program(): step = lambda a: lax.ppermute(a, ('expert', 'blk'), perm)  22.6 us
    ppermute x6, waiting for transfers between devices, square_program(): lax.ppermute(a, 'expert', [(i, i ^ 2 * k) for i in range(groups)])  19.2 us
    ppermute x6, starting transfers between devices, square_program(): lax.ppermute(a, 'expert', [(i, i ^ 2 * k) for i in range(groups)])  12.6 us
    pallas_call x12, Pallas kernels, down_of(): pl.pallas_call(lambda *refs: down_kernel(j, *refs), in_specs=[SMEM] + [VM...  11.1 us
    pallas_call x4, Pallas kernels, hidden_of(): pl.pallas_call(hidden_kernel, in_specs=[SMEM] + [VMEM] * 7, out_specs=[VM...  10.6 us
    unnamed x21, local copies, waits for them, and re-layouts  6.25 us
    ppermute x5, waiting for transfers between devices, square_program(): lax.ppermute(a, 'expert', [(i, i ^ 1) for i in range(groups)])  3.8 us
  transfers between devices with their start and end apart: 35, of which 26 were waited for; matrix products, arithmetic and copies ran while one was open for 1% of the time, Pallas kernels for 15%

profile of v3, /device:TPU:0, one launch (start us, length us, event | category | flops | bytes accessed | tf_op | source)
XLA Modules:
  0.0 143.1 jit_solution(13923433779684920186)
XLA Ops:
  3.4 1.7 %collective-permute-done = bf16[4,96,896]{2,1,0:T(8,128)(2,1)S(1)} collective-permute-done((bf16[4,96,896]{2,1,0:T(8,128)(2,1)S(1)}, bf16[4,96,896]{2,1,0:T(8,128)(2,1)S(1)}, u32[]{:S(2)}, u32[]{:S(2)}) %collective-permute-start) | collective-permute-done | bytes 688160 | tf_op jit(solution)/shard_map/ppermute | solution.py:126
  5.2 3.0 %collective-permute-start.2 = (bf16[192,896]{1,0:T(8,128)(2,1)S(1)}, bf16[192,896]{1,0:T(8,128)(2,1)S(1)}, u32[]{:S(2)}, u32[]{:S(2)}) collective-permute-start(bf16[192,896]{1,0:T(8,128)(2,1)S(1)} %pad_maximum_fusion.1), channel_id=1, source_target_pairs={{0,8},{4,12},{8,0},{12,4},{16,24},{20,28},{24,16},{28,20},{1,9},{5... | collective-permute-start | bytes 1032200 | tf_op jit(solution)/shard_map/ppermute | solution.py:127
  10.5 6.1 %collective-permute-done.2.x0 = bf16[192,896]{1,0:T(8,128)(2,1)S(1)} collective-permute-done((bf16[192,896]{1,0:T(8,128)(2,1)S(1)}, bf16[192,896]{1,0:T(8,128)(2,1)S(1)}, u32[]{:S(2)}, u32[]{:S(2)}) %collective-permute-start.2) | collective-permute-done | bytes 344096 | tf_op jit(solution)/shard_map/ppermute | solution.py:127
  18.2 2.7 %collective-permute-start.4 = (bf16[192,896]{1,0:T(8,128)(2,1)S(1)}, bf16[192,896]{1,0:T(8,128)(2,1)S(1)}, u32[]{:S(2)}, u32[]{:S(2)}) collective-permute-start(bf16[192,896]{1,0:T(8,128)(2,1)S(1)} %pad_maximum_fusion.2), channel_id=1, source_target_pairs={{0,16},{4,20},{8,24},{12,28},{16,0},{20,4},{24,8},{28,12},{1,17},{... | collective-permute-start | bytes 1032200 | tf_op jit(solution)/shard_map/ppermute | solution.py:127
  22.4 2.0 %copy-done.1 = bf16[1,512,3584]{2,1,0:T(8,128)(2,1)S(1)} copy-done((bf16[1,512,3584]{2,1,0:T(8,128)(2,1)S(1)}, bf16[1,512,3584]{2,1,0:T(8,128)(2,1)}, u32[]{:S(2)}) %copy-start.1) | copy-done | bytes 3670040
  24.5 2.0 %copy-done.3 = bf16[1,3584,512]{2,1,0:T(8,128)(2,1)S(1)} copy-done((bf16[1,3584,512]{2,1,0:T(8,128)(2,1)S(1)}, bf16[1,3584,512]{2,1,0:T(8,128)(2,1)}, u32[]{:S(2)}) %copy-start.3) | copy-done | bytes 3670040
  26.5 2.0 %copy-done.5 = bf16[1,3584,512]{2,1,0:T(8,128)(2,1)S(1)} copy-done((bf16[1,3584,512]{2,1,0:T(8,128)(2,1)S(1)}, bf16[1,3584,512]{2,1,0:T(8,128)(2,1)}, u32[]{:S(2)}) %copy-start.5) | copy-done | bytes 3670040
  30.3 5.3 %collective-permute-done.4.x0 = bf16[192,896]{1,0:T(8,128)(2,1)S(1)} collective-permute-done((bf16[192,896]{1,0:T(8,128)(2,1)S(1)}, bf16[192,896]{1,0:T(8,128)(2,1)S(1)}, u32[]{:S(2)}, u32[]{:S(2)}) %collective-permute-start.4) | collective-permute-done | bytes 344096 | tf_op jit(solution)/shard_map/ppermute | solution.py:127
  37.6 5.2 %collective-permute-done.7.x1 = bf16[192,896]{1,0:T(8,128)(2,1)S(1)} collective-permute-done((bf16[192,896]{1,0:T(8,128)(2,1)S(1)}, bf16[192,896]{1,0:T(8,128)(2,1)S(1)}, u32[]{:S(2)}, u32[]{:S(2)}) %collective-permute-start.7) | collective-permute-done | bytes 344096 | tf_op jit(solution)/shard_map/chunk2/ppermute | solution.py:129
  43.5 3.4 %collective-permute-start.11 = (bf16[192,896]{1,0:T(8,128)(2,1)S(1)}, bf16[192,896]{1,0:T(8,128)(2,1)S(1)}, u32[]{:S(2)}, u32[]{:S(2)}) collective-permute-start(bf16[192,896]{1,0:T(8,128)(2,1)S(1)} %pad_maximum_fusion.3), channel_id=1, source_target_pairs={{0,24},{4,28},{8,16},{12,20},{16,8},{20,12},{24,0},{28,4},{1,25},{... | collective-permute-start | bytes 1032200 | tf_op jit(solution)/shard_map/ppermute | solution.py:127
  46.9 3.3 %collective-permute-done.9.x2 = bf16[192,896]{1,0:T(8,128)(2,1)S(1)} collective-permute-done((bf16[192,896]{1,0:T(8,128)(2,1)S(1)}, bf16[192,896]{1,0:T(8,128)(2,1)S(1)}, u32[]{:S(2)}, u32[]{:S(2)}) %collective-permute-start.9) | collective-permute-done | bytes 344096 | tf_op jit(solution)/shard_map/chunk2/ppermute | solution.py:129
  52.2 2.7 %chunk1.4 = (bf16[192,512]{1,0:T(8,128)(2,1)S(1)}, bf16[192,896]{1,0:T(8,128)(2,1)S(1)}) custom-call(s32[4]{0:T(128)S(1)} %shard_map.73.order.refs_0_, bf16[192,896]{1,0:T(8,128)(2,1)S(1)} %collective-permute-done.2.x0, bf16[192,896]{1,0:T(8,128)(2,1)S(1)} %collective-permute-done.5.x1, bf16[192,896]{1,0:T(8,128)(2,1)S(1)} %collective-permute-done.8.x2, ...), custom_call_target="tpu_custom_call" | custom-call | flops 1 | bytes 1 | tf_op jit(solution)/shard_map/chunk1/pallas_call | solution.py:70
  57.5 2.6 %chunk2.4 = (bf16[192,512]{1,0:T(8,128)(2,1)S(1)}, bf16[192,896]{1,0:T(8,128)(2,1)S(1)}) custom-call(s32[4]{0:T(128)S(1)} %shard_map.73.order.refs_0_, bf16[192,896]{1,0:T(8,128)(2,1)S(1)} %collective-permute-done.4.x0, bf16[192,896]{1,0:T(8,128)(2,1)S(1)} %collective-permute-done.7.x1, bf16[192,896]{1,0:T(8,128)(2,1)S(1)} %collective-permute-done.9.x2, ...), custom_call_target="tpu_custom_call" | custom-call | flops 1 | bytes 1 | tf_op jit(solution)/shard_map/chunk2/pallas_call | solution.py:70
  61.2 3.7 %collective-permute-done.15.refs_2_ = bf16[192,896]{1,0:T(8,128)(2,1)S(1)} collective-permute-done((bf16[192,896]{1,0:T(8,128)(2,1)S(1)}, bf16[192,896]{1,0:T(8,128)(2,1)S(1)}, u32[]{:S(2)}, u32[]{:S(2)}) %collective-permute-start.15) | collective-permute-done | bytes 344096 | tf_op jit(solution)/shard_map/chunk1/ppermute | solution.py:129
  66.4 2.1 %collective-permute-done.14.x1 = bf16[192,896]{1,0:T(8,128)(2,1)S(1)} collective-permute-done((bf16[192,896]{1,0:T(8,128)(2,1)S(1)}, bf16[192,896]{1,0:T(8,128)(2,1)S(1)}, u32[]{:S(2)}, u32[]{:S(2)}) %collective-permute-start.14) | collective-permute-done | bytes 344096 | tf_op jit(solution)/shard_map/chunk3/ppermute | solution.py:129
  69.2 3.0 %collective-permute-done.17.refs_2_ = bf16[192,896]{1,0:T(8,128)(2,1)S(1)} collective-permute-done((bf16[192,896]{1,0:T(8,128)(2,1)S(1)}, bf16[192,896]{1,0:T(8,128)(2,1)S(1)}, u32[]{:S(2)}, u32[]{:S(2)}) %collective-permute-start.17) | collective-permute-done | bytes 344096 | tf_op jit(solution)/shard_map/chunk2/ppermute | solution.py:129
  73.9 2.0 %collective-permute-done.16.x2 = bf16[192,896]{1,0:T(8,128)(2,1)S(1)} collective-permute-done((bf16[192,896]{1,0:T(8,128)(2,1)S(1)}, bf16[192,896]{1,0:T(8,128)(2,1)S(1)}, u32[]{:S(2)}, u32[]{:S(2)}) %collective-permute-start.16) | collective-permute-done | bytes 344096 | tf_op jit(solution)/shard_map/chunk3/ppermute | solution.py:129
  76.6 3.9 %collective-permute-done.19.refs_2_ = bf16[192,896]{1,0:T(8,128)(2,1)S(1)} collective-permute-done((bf16[192,896]{1,0:T(8,128)(2,1)S(1)}, bf16[192,896]{1,0:T(8,128)(2,1)S(1)}, u32[]{:S(2)}, u32[]{:S(2)}) %collective-permute-start.19) | collective-permute-done | bytes 344096 | tf_op jit(solution)/shard_map/chunk2/ppermute | solution.py:129
  82.1 2.1 %collective-permute-done.18.x3 = bf16[192,896]{1,0:T(8,128)(2,1)S(1)} collective-permute-done((bf16[192,896]{1,0:T(8,128)(2,1)S(1)}, bf16[192,896]{1,0:T(8,128)(2,1)S(1)}, u32[]{:S(2)}, u32[]{:S(2)}) %collective-permute-start.18) | collective-permute-done | bytes 344096 | tf_op jit(solution)/shard_map/chunk3/ppermute | solution.py:129
  84.2 2.7 %chunk3.4 = (bf16[192,512]{1,0:T(8,128)(2,1)S(1)}, bf16[192,896]{1,0:T(8,128)(2,1)S(1)}) custom-call(s32[4]{0:T(128)S(1)} %shard_map.73.order.refs_0_, bf16[192,896]{1,0:T(8,128)(2,1)S(1)} %collective-permute-done.11.x0, bf16[192,896]{1,0:T(8,128)(2,1)S(1)} %collective-permute-done.14.x1, bf16[192,896]{1,0:T(8,128)(2,1)S(1)} %collective-permute-done.16.x2, ...), custom_call_target="tpu_custom_call" | custom-call | flops 1 | bytes 1 | tf_op jit(solution)/shard_map/chunk3/pallas_call | solution.py:70
  89.8 4.3 %collective-permute-done.20.refs_2_ = bf16[192,896]{1,0:T(8,128)(2,1)S(1)} collective-permute-done((bf16[192,896]{1,0:T(8,128)(2,1)S(1)}, bf16[192,896]{1,0:T(8,128)(2,1)S(1)}, u32[]{:S(2)}, u32[]{:S(2)}) %collective-permute-start.20) | collective-permute-done | bytes 344096 | tf_op jit(solution)/shard_map/chunk3/ppermute | solution.py:129
  95.8 2.1 %collective-permute-done.23.refs_2_ = bf16[192,896]{1,0:T(8,128)(2,1)S(1)} collective-permute-done((bf16[192,896]{1,0:T(8,128)(2,1)S(1)}, bf16[192,896]{1,0:T(8,128)(2,1)S(1)}, u32[]{:S(2)}, u32[]{:S(2)}) %collective-permute-start.23) | collective-permute-done | bytes 344096 | tf_op jit(solution)/shard_map/chunk1/ppermute | solution.py:129
  99.5 2.9 %collective-permute-done.22.refs_2_ = bf16[192,896]{1,0:T(8,128)(2,1)S(1)} collective-permute-done((bf16[192,896]{1,0:T(8,128)(2,1)S(1)}, bf16[192,896]{1,0:T(8,128)(2,1)S(1)}, u32[]{:S(2)}, u32[]{:S(2)}) %collective-permute-start.22) | collective-permute-done | bytes 344096 | tf_op jit(solution)/shard_map/chunk3/ppermute | solution.py:129
  104.2 2.7 %chunk0.4 = (bf16[192,512]{1,0:T(8,128)(2,1)S(1)}, bf16[192,896]{1,0:T(8,128)(2,1)S(1)}) custom-call(s32[4]{0:T(128)S(1)} %shard_map.73.order.refs_0_, bf16[192,896]{1,0:T(8,128)(2,1)S(1)} %pad_maximum_fusion.x0, bf16[192,896]{1,0:T(8,128)(2,1)S(1)} %collective-permute-done.1.x1, bf16[192,896]{1,0:T(8,128)(2,1)S(1)} %collective-permute-done.3.x2, ...), custom_call_target="tpu_custom_call" | custom-call | flops 1 | bytes 1 | tf_op jit(solution)/shard_map/chunk0/pallas_call | solution.py:70
  108.3 1.9 %collective-permute-done.26 = bf16[192,896]{1,0:T(8,128)(2,1)S(1)} collective-permute-done((bf16[192,896]{1,0:T(8,128)(2,1)S(1)}, bf16[192,896]{1,0:T(8,128)(2,1)S(1)}, u32[]{:S(2)}, u32[]{:S(2)}) %collective-permute-start.26) | collective-permute-done | bytes 344096 | tf_op jit(solution)/shard_map/chunk2/ppermute | solution.py:127
  112.1 2.4 %collective-permute-done.13.refs_2_ = bf16[192,896]{1,0:T(8,128)(2,1)S(1)} collective-permute-done((bf16[192,896]{1,0:T(8,128)(2,1)S(1)}, bf16[192,896]{1,0:T(8,128)(2,1)S(1)}, u32[]{:S(2)}, u32[]{:S(2)}) %collective-permute-start.13) | collective-permute-done | bytes 344096 | tf_op jit(solution)/shard_map/chunk0/ppermute | solution.py:129
  116.5 6.2 %collective-permute-done.27.refs_2_ = bf16[192,896]{1,0:T(8,128)(2,1)S(1)} collective-permute-done((bf16[192,896]{1,0:T(8,128)(2,1)S(1)}, bf16[192,896]{1,0:T(8,128)(2,1)S(1)}, u32[]{:S(2)}, u32[]{:S(2)}) %collective-permute-start.27) | collective-permute-done | bytes 344096 | tf_op jit(solution)/shard_map/chunk0/ppermute | solution.py:129
  124.7 3.5 %collective-permute-start.31 = (bf16[192,896]{1,0:T(8,128)(2,1)S(1)}, bf16[192,896]{1,0:T(8,128)(2,1)S(1)}, u32[]{:S(2)}, u32[]{:S(2)}) collective-permute-start(bf16[192,896]{1,0:T(8,128)(2,1)S(1)} %chunk3.7), channel_id=1, source_target_pairs={{0,24},{4,28},{8,16},{12,20},{16,8},{20,12},{24,0},{28,4},{1,25},{... | collective-permute-start | bytes 1032200 | tf_op jit(solution)/shard_map/chunk3/ppermute | solution.py:127
  128.3 2.6 %collective-permute-done.28.refs_2_ = bf16[192,896]{1,0:T(8,128)(2,1)S(1)} collective-permute-done((bf16[192,896]{1,0:T(8,128)(2,1)S(1)}, bf16[192,896]{1,0:T(8,128)(2,1)S(1)}, u32[]{:S(2)}, u32[]{:S(2)}) %collective-permute-start.28) | collective-permute-done | bytes 344096 | tf_op jit(solution)/shard_map/chunk0/ppermute | solution.py:129
  131.9 2.2 %collective-permute-done.31 = bf16[192,896]{1,0:T(8,128)(2,1)S(1)} collective-permute-done((bf16[192,896]{1,0:T(8,128)(2,1)S(1)}, bf16[192,896]{1,0:T(8,128)(2,1)S(1)}, u32[]{:S(2)}, u32[]{:S(2)}) %collective-permute-start.31) | collective-permute-done | bytes 344096 | tf_op jit(solution)/shard_map/chunk3/ppermute | solution.py:127
  134.1 3.6 %collective-permute-done.30 = bf16[192,896]{1,0:T(8,128)(2,1)S(1)} collective-permute-done((bf16[192,896]{1,0:T(8,128)(2,1)S(1)}, bf16[192,896]{1,0:T(8,128)(2,1)S(1)}, u32[]{:S(2)}, u32[]{:S(2)}) %collective-permute-start.30) | collective-permute-done | bytes 344096 | tf_op jit(solution)/shard_map/chunk1/ppermute | solution.py:127
  141.1 2.0 %multiply_convert_fusion = bf16[512,896]{1,0:T(8,128)(2,1)} fusion(bf16[768,896]{1,0:T(8,128)(2,1)S(1)} %constant_dynamic-update-slice_fusion, f32[512]{0:T(512)S(1)} %bitcast.59, s32[512]{0:T(512)S(1)} %multiply_add_fusion), kind=kOutput, calls=%fused_computation | convolution fusion | flops 705953792 | bytes 2297856 | tf_op jit(solution)/shard_map/dot_general | solution.py:180
  (93 shorter events, 44.8 us)
Async XLA Ops:
  2.8 2.3 %collective-permute-start = (bf16[4,96,896]{2,1,0:T(8,128)(2,1)S(1)}, bf16[4,96,896]{2,1,0:T(8,128)(2,1)S(1)}, u32[]{:S(2)}, u32[]{:S(2)}) collective-permute-start(bf16[4,96,896]{2,1,0:T(8,128)(2,1)S(1)} %slice_bitcast_fusion), channel_id=1, source_target_pairs={{0,4},{4,0},{8,12},{12,8},{16,20},{20,16},{24,28},{28,24},{1,5},{5... | collective-permute-start | bytes 2064392 | tf_op jit(solution)/shard_map/ppermute | solution.py:126
  5.2 11.4 %collective-permute-start.2 = (bf16[192,896]{1,0:T(8,128)(2,1)S(1)}, bf16[192,896]{1,0:T(8,128)(2,1)S(1)}, u32[]{:S(2)}, u32[]{:S(2)}) collective-permute-start(bf16[192,896]{1,0:T(8,128)(2,1)S(1)} %pad_maximum_fusion.1), channel_id=1, source_target_pairs={{0,8},{4,12},{8,0},{12,4},{16,24},{20,28},{24,16},{28,20},{1,9},{5... | collective-permute-start | bytes 1032200 | tf_op jit(solution)/shard_map/ppermute | solution.py:127
  8.9 12.0 %collective-permute-start.1 = (bf16[192,896]{1,0:T(8,128)(2,1)S(1)}, bf16[192,896]{1,0:T(8,128)(2,1)S(1)}, u32[]{:S(2)}, u32[]{:S(2)}) collective-permute-start(bf16[192,896]{1,0:T(8,128)(2,1)S(1)} %pad_maximum_fusion.x0), channel_id=1, source_target_pairs={{0,1},{1,3},{3,2},{2,0},{4,6},{5,4},{7,5},{6,7},{8,9},{9,11},{11,1... | collective-permute-start | bytes 1032200 | tf_op jit(solution)/shard_map/ppermute | solution.py:129
  16.6 13.1 %collective-permute-start.5 = (bf16[192,896]{1,0:T(8,128)(2,1)S(1)}, bf16[192,896]{1,0:T(8,128)(2,1)S(1)}, u32[]{:S(2)}, u32[]{:S(2)}) collective-permute-start(bf16[192,896]{1,0:T(8,128)(2,1)S(1)} %collective-permute-done.2.x0), channel_id=1, source_target_pairs={{0,1},{1,3},{3,2},{2,0},{4,6},{5,4},{7,5},{6,7},{8,9},{9,11},{11,1... | collective-permute-start | bytes 1032200 | tf_op jit(solution)/shard_map/chunk1/ppermute | solution.py:129
  18.2 17.4 %collective-permute-start.4 = (bf16[192,896]{1,0:T(8,128)(2,1)S(1)}, bf16[192,896]{1,0:T(8,128)(2,1)S(1)}, u32[]{:S(2)}, u32[]{:S(2)}) collective-permute-start(bf16[192,896]{1,0:T(8,128)(2,1)S(1)} %pad_maximum_fusion.2), channel_id=1, source_target_pairs={{0,16},{4,20},{8,24},{12,28},{16,0},{20,4},{24,8},{28,12},{1,17},{... | collective-permute-start | bytes 1032200 | tf_op jit(solution)/shard_map/ppermute | solution.py:127
  20.9 15.4 %collective-permute-start.3 = (bf16[192,896]{1,0:T(8,128)(2,1)S(1)}, bf16[192,896]{1,0:T(8,128)(2,1)S(1)}, u32[]{:S(2)}, u32[]{:S(2)}) collective-permute-start(bf16[192,896]{1,0:T(8,128)(2,1)S(1)} %collective-permute-done.1.x1), channel_id=1, source_target_pairs={{0,1},{1,3},{3,2},{2,0},{4,6},{5,4},{7,5},{6,7},{8,9},{9,11},{11,1... | collective-permute-start | bytes 1032200 | tf_op jit(solution)/shard_map/chunk0/ppermute | solution.py:129
  29.7 7.3 %collective-permute-start.8 = (bf16[192,896]{1,0:T(8,128)(2,1)S(1)}, bf16[192,896]{1,0:T(8,128)(2,1)S(1)}, u32[]{:S(2)}, u32[]{:S(2)}) collective-permute-start(bf16[192,896]{1,0:T(8,128)(2,1)S(1)} %collective-permute-done.5.x1), channel_id=1, source_target_pairs={{0,1},{1,3},{3,2},{2,0},{4,6},{5,4},{7,5},{6,7},{8,9},{9,11},{11,1... | collective-permute-start | bytes 1032200 | tf_op jit(solution)/shard_map/chunk1/ppermute | solution.py:129
  35.6 7.2 %collective-permute-start.7 = (bf16[192,896]{1,0:T(8,128)(2,1)S(1)}, bf16[192,896]{1,0:T(8,128)(2,1)S(1)}, u32[]{:S(2)}, u32[]{:S(2)}) collective-permute-start(bf16[192,896]{1,0:T(8,128)(2,1)S(1)} %collective-permute-done.4.x0), channel_id=1, source_target_pairs={{0,1},{1,3},{3,2},{2,0},{4,6},{5,4},{7,5},{6,7},{8,9},{9,11},{11,1... | collective-permute-start | bytes 1032200 | tf_op jit(solution)/shard_map/chunk2/ppermute | solution.py:129
  37.0 15.2 %collective-permute-start.12 = (bf16[192,896]{1,0:T(8,128)(2,1)S(1)}, bf16[192,896]{1,0:T(8,128)(2,1)S(1)}, u32[]{:S(2)}, u32[]{:S(2)}) collective-permute-start(bf16[192,896]{1,0:T(8,128)(2,1)S(1)} %collective-permute-done.8.x2), channel_id=1, source_target_pairs={{0,1},{1,3},{3,2},{2,0},{4,6},{5,4},{7,5},{6,7},{8,9},{9,11},{11,1... | collective-permute-start | bytes 1032200 | tf_op jit(solution)/shard_map/chunk1/ppermute | solution.py:129
  42.9 7.4 %collective-permute-start.9 = (bf16[192,896]{1,0:T(8,128)(2,1)S(1)}, bf16[192,896]{1,0:T(8,128)(2,1)S(1)}, u32[]{:S(2)}, u32[]{:S(2)}) collective-permute-start(bf16[192,896]{1,0:T(8,128)(2,1)S(1)} %collective-permute-done.7.x1), channel_id=1, source_target_pairs={{0,1},{1,3},{3,2},{2,0},{4,6},{5,4},{7,5},{6,7},{8,9},{9,11},{11,1... | collective-permute-start | bytes 1032200 | tf_op jit(solution)/shard_map/chunk2/ppermute | solution.py:129
  43.5 12.9 %collective-permute-start.11 = (bf16[192,896]{1,0:T(8,128)(2,1)S(1)}, bf16[192,896]{1,0:T(8,128)(2,1)S(1)}, u32[]{:S(2)}, u32[]{:S(2)}) collective-permute-start(bf16[192,896]{1,0:T(8,128)(2,1)S(1)} %pad_maximum_fusion.3), channel_id=1, source_target_pairs={{0,24},{4,28},{8,16},{12,20},{16,8},{20,12},{24,0},{28,4},{1,25},{... | collective-permute-start | bytes 1032200 | tf_op jit(solution)/shard_map/ppermute | solution.py:127
  50.2 7.2 %collective-permute-start.10 = (bf16[192,896]{1,0:T(8,128)(2,1)S(1)}, bf16[192,896]{1,0:T(8,128)(2,1)S(1)}, u32[]{:S(2)}, u32[]{:S(2)}) collective-permute-start(bf16[192,896]{1,0:T(8,128)(2,1)S(1)} %collective-permute-done.9.x2), channel_id=1, source_target_pairs={{0,1},{1,3},{3,2},{2,0},{4,6},{5,4},{7,5},{6,7},{8,9},{9,11},{11,1... | collective-permute-start | bytes 1032200 | tf_op jit(solution)/shard_map/chunk2/ppermute | solution.py:129
  50.9 10.3 %collective-permute-start.6 = (bf16[192,896]{1,0:T(8,128)(2,1)S(1)}, bf16[192,896]{1,0:T(8,128)(2,1)S(1)}, u32[]{:S(2)}, u32[]{:S(2)}) collective-permute-start(bf16[192,896]{1,0:T(8,128)(2,1)S(1)} %collective-permute-done.3.x2), channel_id=1, source_target_pairs={{0,1},{1,3},{3,2},{2,0},{4,6},{5,4},{7,5},{6,7},{8,9},{9,11},{11,1... | collective-permute-start | bytes 1032200 | tf_op jit(solution)/shard_map/chunk0/ppermute | solution.py:129
  54.9 9.9 %collective-permute-start.15 = (bf16[192,896]{1,0:T(8,128)(2,1)S(1)}, bf16[192,896]{1,0:T(8,128)(2,1)S(1)}, u32[]{:S(2)}, u32[]{:S(2)}) collective-permute-start(bf16[192,896]{1,0:T(8,128)(2,1)S(1)} %get-tuple-element.64), channel_id=1, source_target_pairs={{0,1},{1,3},{3,2},{2,0},{4,6},{5,4},{7,5},{6,7},{8,9},{9,11},{11,1... | collective-permute-start | bytes 1032200 | tf_op jit(solution)/shard_map/chunk1/ppermute | solution.py:129
  56.5 12.1 %collective-permute-start.14 = (bf16[192,896]{1,0:T(8,128)(2,1)S(1)}, bf16[192,896]{1,0:T(8,128)(2,1)S(1)}, u32[]{:S(2)}, u32[]{:S(2)}) collective-permute-start(bf16[192,896]{1,0:T(8,128)(2,1)S(1)} %collective-permute-done.11.x0), channel_id=1, source_target_pairs={{0,1},{1,3},{3,2},{2,0},{4,6},{5,4},{7,5},{6,7},{8,9},{9,11},{11,1... | collective-permute-start | bytes 1032200 | tf_op jit(solution)/shard_map/chunk3/ppermute | solution.py:129
  64.9 7.4 %collective-permute-start.17 = (bf16[192,896]{1,0:T(8,128)(2,1)S(1)}, bf16[192,896]{1,0:T(8,128)(2,1)S(1)}, u32[]{:S(2)}, u32[]{:S(2)}) collective-permute-start(bf16[192,896]{1,0:T(8,128)(2,1)S(1)} %get-tuple-element.68), channel_id=1, source_target_pairs={{0,1},{1,3},{3,2},{2,0},{4,6},{5,4},{7,5},{6,7},{8,9},{9,11},{11,1... | collective-permute-start | bytes 1032200 | tf_op jit(solution)/shard_map/chunk2/ppermute | solution.py:129
  68.5 7.4 %collective-permute-start.16 = (bf16[192,896]{1,0:T(8,128)(2,1)S(1)}, bf16[192,896]{1,0:T(8,128)(2,1)S(1)}, u32[]{:S(2)}, u32[]{:S(2)}) collective-permute-start(bf16[192,896]{1,0:T(8,128)(2,1)S(1)} %collective-permute-done.14.x1), channel_id=1, source_target_pairs={{0,1},{1,3},{3,2},{2,0},{4,6},{5,4},{7,5},{6,7},{8,9},{9,11},{11,1... | collective-permute-start | bytes 1032200 | tf_op jit(solution)/shard_map/chunk3/ppermute | solution.py:129
  73.2 7.3 %collective-permute-start.19 = (bf16[192,896]{1,0:T(8,128)(2,1)S(1)}, bf16[192,896]{1,0:T(8,128)(2,1)S(1)}, u32[]{:S(2)}, u32[]{:S(2)}) collective-permute-start(bf16[192,896]{1,0:T(8,128)(2,1)S(1)} %chunk2.5), channel_id=1, source_target_pairs={{0,1},{1,3},{3,2},{2,0},{4,6},{5,4},{7,5},{6,7},{8,9},{9,11},{11,1... | collective-permute-start | bytes 1032200 | tf_op jit(solution)/shard_map/chunk2/ppermute | solution.py:129
  75.9 8.3 %collective-permute-start.18 = (bf16[192,896]{1,0:T(8,128)(2,1)S(1)}, bf16[192,896]{1,0:T(8,128)(2,1)S(1)}, u32[]{:S(2)}, u32[]{:S(2)}) collective-permute-start(bf16[192,896]{1,0:T(8,128)(2,1)S(1)} %collective-permute-done.16.x2), channel_id=1, source_target_pairs={{0,1},{1,3},{3,2},{2,0},{4,6},{5,4},{7,5},{6,7},{8,9},{9,11},{11,1... | collective-permute-start | bytes 1032200 | tf_op jit(solution)/shard_map/chunk3/ppermute | solution.py:129
  81.4 7.5 %collective-permute-start.21 = (bf16[192,896]{1,0:T(8,128)(2,1)S(1)}, bf16[192,896]{1,0:T(8,128)(2,1)S(1)}, u32[]{:S(2)}, u32[]{:S(2)}) collective-permute-start(bf16[192,896]{1,0:T(8,128)(2,1)S(1)} %chunk2.6), channel_id=1, source_target_pairs={{0,1},{1,3},{3,2},{2,0},{4,6},{5,4},{7,5},{6,7},{8,9},{9,11},{11,1... | collective-permute-start | bytes 1032200 | tf_op jit(solution)/shard_map/chunk2/ppermute | solution.py:129
  86.8 7.3 %collective-permute-start.20 = (bf16[192,896]{1,0:T(8,128)(2,1)S(1)}, bf16[192,896]{1,0:T(8,128)(2,1)S(1)}, u32[]{:S(2)}, u32[]{:S(2)}) collective-permute-start(bf16[192,896]{1,0:T(8,128)(2,1)S(1)} %get-tuple-element.74), channel_id=1, source_target_pairs={{0,1},{1,3},{3,2},{2,0},{4,6},{5,4},{7,5},{6,7},{8,9},{9,11},{11,1... | collective-permute-start | bytes 1032200 | tf_op jit(solution)/shard_map/chunk3/ppermute | solution.py:129
  87.5 10.3 %collective-permute-start.23 = (bf16[192,896]{1,0:T(8,128)(2,1)S(1)}, bf16[192,896]{1,0:T(8,128)(2,1)S(1)}, u32[]{:S(2)}, u32[]{:S(2)}) collective-permute-start(bf16[192,896]{1,0:T(8,128)(2,1)S(1)} %chunk1.5), channel_id=1, source_target_pairs={{0,1},{1,3},{3,2},{2,0},{4,6},{5,4},{7,5},{6,7},{8,9},{9,11},{11,1... | collective-permute-start | bytes 1032200 | tf_op jit(solution)/shard_map/chunk1/ppermute | solution.py:129
  95.1 7.3 %collective-permute-start.22 = (bf16[192,896]{1,0:T(8,128)(2,1)S(1)}, bf16[192,896]{1,0:T(8,128)(2,1)S(1)}, u32[]{:S(2)}, u32[]{:S(2)}) collective-permute-start(bf16[192,896]{1,0:T(8,128)(2,1)S(1)} %chunk3.5), channel_id=1, source_target_pairs={{0,1},{1,3},{3,2},{2,0},{4,6},{5,4},{7,5},{6,7},{8,9},{9,11},{11,1... | collective-permute-start | bytes 1032200 | tf_op jit(solution)/shard_map/chunk3/ppermute | solution.py:129
  95.8 14.4 %collective-permute-start.26 = (bf16[192,896]{1,0:T(8,128)(2,1)S(1)}, bf16[192,896]{1,0:T(8,128)(2,1)S(1)}, u32[]{:S(2)}, u32[]{:S(2)}) collective-permute-start(bf16[192,896]{1,0:T(8,128)(2,1)S(1)} %chunk2.7), channel_id=1, source_target_pairs={{0,16},{4,20},{8,24},{12,28},{16,0},{20,4},{24,8},{28,12},{1,17},{... | collective-permute-start | bytes 1032200 | tf_op jit(solution)/shard_map/chunk2/ppermute | solution.py:127
  98.8 11.4 %collective-permute-start.25 = (bf16[192,896]{1,0:T(8,128)(2,1)S(1)}, bf16[192,896]{1,0:T(8,128)(2,1)S(1)}, u32[]{:S(2)}, u32[]{:S(2)}) collective-permute-start(bf16[192,896]{1,0:T(8,128)(2,1)S(1)} %chunk1.6), channel_id=1, source_target_pairs={{0,1},{1,3},{3,2},{2,0},{4,6},{5,4},{7,5},{6,7},{8,9},{9,11},{11,1... | collective-permute-start | bytes 1032200 | tf_op jit(solution)/shard_map/chunk1/ppermute | solution.py:129
  103.3 7.8 %collective-permute-start.24 = (bf16[192,896]{1,0:T(8,128)(2,1)S(1)}, bf16[192,896]{1,0:T(8,128)(2,1)S(1)}, u32[]{:S(2)}, u32[]{:S(2)}) collective-permute-start(bf16[192,896]{1,0:T(8,128)(2,1)S(1)} %chunk3.6), channel_id=1, source_target_pairs={{0,1},{1,3},{3,2},{2,0},{4,6},{5,4},{7,5},{6,7},{8,9},{9,11},{11,1... | collective-permute-start | bytes 1032200 | tf_op jit(solution)/shard_map/chunk3/ppermute | solution.py:129
  106.8 7.6 %collective-permute-start.13 = (bf16[192,896]{1,0:T(8,128)(2,1)S(1)}, bf16[192,896]{1,0:T(8,128)(2,1)S(1)}, u32[]{:S(2)}, u32[]{:S(2)}) collective-permute-start(bf16[192,896]{1,0:T(8,128)(2,1)S(1)} %get-tuple-element.62), channel_id=1, source_target_pairs={{0,1},{1,3},{3,2},{2,0},{4,6},{5,4},{7,5},{6,7},{8,9},{9,11},{11,1... | collective-permute-start | bytes 1032200 | tf_op jit(solution)/shard_map/chunk0/ppermute | solution.py:129
  115.4 7.3 %collective-permute-start.27 = (bf16[192,896]{1,0:T(8,128)(2,1)S(1)}, bf16[192,896]{1,0:T(8,128)(2,1)S(1)}, u32[]{:S(2)}, u32[]{:S(2)}) collective-permute-start(bf16[192,896]{1,0:T(8,128)(2,1)S(1)} %chunk0.5), channel_id=1, source_target_pairs={{0,1},{1,3},{3,2},{2,0},{4,6},{5,4},{7,5},{6,7},{8,9},{9,11},{11,1... | collective-permute-start | bytes 1032200 | tf_op jit(solution)/shard_map/chunk0/ppermute | solution.py:129
  123.6 7.3 %collective-permute-start.28 = (bf16[192,896]{1,0:T(8,128)(2,1)S(1)}, bf16[192,896]{1,0:T(8,128)(2,1)S(1)}, u32[]{:S(2)}, u32[]{:S(2)}) collective-permute-start(bf16[192,896]{1,0:T(8,128)(2,1)S(1)} %chunk0.6), channel_id=1, source_target_pairs={{0,1},{1,3},{3,2},{2,0},{4,6},{5,4},{7,5},{6,7},{8,9},{9,11},{11,1... | collective-permute-start | bytes 1032200 | tf_op jit(solution)/shard_map/chunk0/ppermute | solution.py:129
  124.7 9.4 %collective-permute-start.31 = (bf16[192,896]{1,0:T(8,128)(2,1)S(1)}, bf16[192,896]{1,0:T(8,128)(2,1)S(1)}, u32[]{:S(2)}, u32[]{:S(2)}) collective-permute-start(bf16[192,896]{1,0:T(8,128)(2,1)S(1)} %chunk3.7), channel_id=1, source_target_pairs={{0,24},{4,28},{8,16},{12,20},{16,8},{20,12},{24,0},{28,4},{1,25},{... | collective-permute-start | bytes 1032200 | tf_op jit(solution)/shard_map/chunk3/ppermute | solution.py:127
  128.2 9.5 %collective-permute-start.30 = (bf16[192,896]{1,0:T(8,128)(2,1)S(1)}, bf16[192,896]{1,0:T(8,128)(2,1)S(1)}, u32[]{:S(2)}, u32[]{:S(2)}) collective-permute-start(bf16[192,896]{1,0:T(8,128)(2,1)S(1)} %chunk1.7), channel_id=1, source_target_pairs={{0,8},{4,12},{8,0},{12,4},{16,24},{20,28},{24,16},{28,20},{1,9},{5... | collective-permute-start | bytes 1032200 | tf_op jit(solution)/shard_map/chunk1/ppermute | solution.py:127
  128.2 10.2 %collective-permute-start.33 = (bf16[96,896]{1,0:T(8,128)(2,1)S(1)}, bf16[96,896]{1,0:T(8,128)(2,1)S(1)}, u32[]{:S(2)}, u32[]{:S(2)}) collective-permute-start(bf16[96,896]{1,0:T(8,128)(2,1)S(1)} %slice.63), channel_id=1, source_target_pairs={{0,4},{4,0},{8,12},{12,8},{16,20},{20,16},{24,28},{28,24},{1,5},{5... | collective-permute-start | bytes 516104 | tf_op jit(solution)/shard_map/chunk2/ppermute | solution.py:126
  (11 other events, 72.5 us)

commit v4 on v3

--- a/solution.py
+++ b/solution.py
@@ -43,24 +43,108 @@
 
 SMEM = pl.BlockSpec(memory_space=pltpu.SMEM)
 VMEM = pl.BlockSpec(memory_space=pltpu.VMEM)
+HBM = pl.BlockSpec(memory_space=pltpu.HBM)
 COST = pl.CostEstimate(flops=1, bytes_accessed=1, transcendentals=0)
+LONG = pl.CostEstimate(flops=10**11, bytes_accessed=1, transcendentals=0)
 LIMIT = pltpu.CompilerParams(vmem_limit_bytes=12 * 1024 * 1024)
 
 
-def order_kernel(order, wg, wu, wd, out):
+def across(row, lanes):
+    return jnp.broadcast_to(row, (lanes, row.shape[1])).T
+
+
+def dispatch_kernel(capacity, at, route, tokens, even, odd, ids, order):
+    me, place = at[0], at[1]
     for j in range(order.shape[0]):
-        out[j] = order[j]
-
-
-def order_of(order, wg, wu, wd):
-    return pl.pallas_call(
-        order_kernel,
-        in_specs=[SMEM] + [VMEM] * 3,
-        out_specs=SMEM,
-        out_shape=jax.ShapeDtypeStruct(order.shape, order.dtype),
+        way = jnp.where(me & 1 == 0, -j, j)
+        number = ((place ^ (place >> 1)) + way) & (order.shape[0] - 1)
+        order[j] = number ^ (number >> 1)
+    count = tokens.shape[0]
+    groups = 2 * even.shape[0] // capacity
+    row = route[...]
+    column = across(row.astype(jnp.float32), 128)[:, :1].astype(jnp.int32)
+    first = lax.broadcasted_iota(jnp.int32, (count, count), 0)
+    second = lax.broadcasted_iota(jnp.int32, (count, count), 1)
+    earlier = jnp.where((column == row) & (first < second), 1.0, 0.0)
+    rank = jnp.sum(earlier, axis=0, keepdims=True).astype(jnp.int32)
+    relative = row ^ me
+    own = ((relative & 1) * (groups // 2) + (relative >> 1)) * capacity + rank
+    ids[...] = own
+    slots = lax.broadcasted_iota(jnp.int32, (groups * capacity, count), 0)
+    selector = jnp.where(slots == own, 1.0, 0.0).astype(jnp.bfloat16)
+    rows = jnp.dot(selector, tokens[...], preferred_element_type=jnp.float32).astype(jnp.bfloat16)
+    even[...] = rows[: even.shape[0]]
+    odd[...] = rows[even.shape[0] :]
+
+
+def dispatch(me, place, route, tokens, groups, capacity):
+    count, width = tokens.shape
+    half = jax.ShapeDtypeStruct((groups * capacity // 2, width), tokens.dtype)
+    return pl.pallas_call(
+        lambda *refs: dispatch_kernel(capacity, *refs),
+        in_specs=[SMEM, VMEM, VMEM],
+        out_specs=[VMEM] * 3 + [SMEM],
+        out_shape=[
+            half,
+            half,
+            jax.ShapeDtypeStruct((1, count), jnp.int32),
+            jax.ShapeDtypeStruct((len(RING),), jnp.int32),
+        ],
+        compiler_params=LIMIT,
+        cost_estimate=LONG,
+    )(jnp.stack([me, place]), route.reshape(1, count), tokens)
+
+
+def combine_kernel(ids, score, *refs):
+    *pieces, out, rows = refs
+    count, capacity = out.shape[0], pieces[-1].shape[0]
+    half = len(pieces) // 2
+    for k in range(half):
+        rows[k * capacity : (k + 1) * capacity] = pieces[k][:capacity]
+        rows[(half + k) * capacity : (half + k + 1) * capacity] = pieces[half + k][...]
+    column = across(ids[...].astype(jnp.float32), 128)[:, :1].astype(jnp.int32)
+    slots = lax.broadcasted_iota(jnp.int32, (count, rows.shape[0]), 1)
+    selector = jnp.where(slots == column, 1.0, 0.0).astype(jnp.bfloat16)
+    picked = jnp.dot(selector, rows[...], preferred_element_type=jnp.float32)
+    out[...] = (picked * across(score[...], 128)[:, :1]).astype(jnp.bfloat16)
+
+
+def combine(ids, score, mine, theirs):
+    count, (capacity, width) = ids.shape[1], theirs[0].shape
+    return pl.pallas_call(
+        combine_kernel,
+        in_specs=[VMEM] * (2 + 2 * len(mine)),
+        out_specs=VMEM,
+        out_shape=jax.ShapeDtypeStruct((count, width), jnp.bfloat16),
+        scratch_shapes=[pltpu.VMEM((2 * len(mine) * capacity, width), jnp.bfloat16)],
         compiler_params=LIMIT,
         cost_estimate=COST,
-    )(order, wg, wu, wd)
+    )(ids, score.reshape(1, count), *mine, *theirs)
+
+
+def load_kernel(order, wg, wu, wd, order_out, wg_out, wu_out, wd_out, done):
+    copies = [
+        pltpu.make_async_copy(source, target, done.at[i])
+        for i, (source, target) in enumerate(((wg, wg_out), (wu, wu_out), (wd, wd_out)))
+    ]
+    for copy in copies:
+        copy.start()
+    for j in range(order.shape[0]):
+        order_out[j] = order[j]
+    for copy in copies:
+        copy.wait()
+
+
+def load(order, *weights):
+    return pl.pallas_call(
+        load_kernel,
+        in_specs=[SMEM] + [HBM] * 3,
+        out_specs=[SMEM] + [VMEM] * 3,
+        out_shape=[jax.ShapeDtypeStruct(a.shape, a.dtype) for a in (order, *weights)],
+        scratch_shapes=[pltpu.SemaphoreType.DMA((3,))],
+        compiler_params=LIMIT,
+        cost_estimate=COST,
+    )(order, *weights)
 
 
 def hidden_of(order, xs, wg, wu, wd):
@@ -106,54 +190,52 @@
     return lax.optimization_barrier((value, *done))[0]
 
 
+TURNS = (0, 3, 0, 1, 3, 3, 1, 2, 0, 3, 1, 2, 1, 2, 0, 3, 2, 1, 3, 2, 1, 3, 2, 1, 0, 3, 2, 1, 0, 0, 2, 0, 1, 3, 2)
+
+HALVES = ()
+LOAD_AT = 3
+
+
 def turns_of(chunks):
     return TURNS if chunks == 4 else [k for _ in range(9) for k in range(chunks)]
-
-
-TURNS = (1, 0, 1, 2, 0, 1, 2, 2, 1, 3, 2, 0, 1, 3, 2, 3, 2, 3, 2, 3, 1, 3, 2, 1, 3, 0, 0, 0, 3, 1, 2, 1, 0, 3)
 
 
 def square_program(tokens, route, gate_score, wg, wu, wd, capacity):
     groups, n = lax.axis_size("expert"), lax.axis_size("blk")
     me, place = lax.axis_index("expert"), lax.axis_index("blk")
-    target = route[:, 0]
-    relative = target ^ me
-    slot_ids = relative * capacity + rank_of(target)
-    selector = selector_of(slot_ids, groups * capacity)
-    outgoing = jnp.dot(selector, tokens, preferred_element_type=jnp.float32).astype(jnp.bfloat16)
     chunks, width = groups // 2, tokens.shape[1]
-    outgoing = outgoing.reshape(chunks, 2, capacity, width)
     sibling = lambda a: lax.ppermute(a, "expert", [(i, i ^ 1) for i in range(groups)])
     other = lambda a, k: lax.ppermute(a, "expert", [(i, i ^ (2 * k)) for i in range(groups)])
     perm = ring_perm(groups, n)
     step = lambda a: lax.ppermute(a, ("expert", "blk"), perm)
-    forward = {RING[i]: [RING[(i - s) % n] for s in range(n)] for i in range(n)}
-    backward = {RING[i]: [RING[(i + s) % n] for s in range(n)] for i in range(n)}
-    table = jnp.array([[forward[i] for i in range(n)], [backward[i] for i in range(n)]], jnp.int32)
-    order = table[me % 2, place]
-
-    swapped = sibling(outgoing[:, 1])
-    packed = [jnp.concatenate([outgoing[k, 0], swapped[k]], 0) for k in range(chunks)]
+    even, odd, ids, order = dispatch(me, place, route, tokens, groups, capacity)
+    swapped = sibling(odd)
+    part_of = lambda a, k: a[k * capacity : (k + 1) * capacity]
+    packed = [jnp.concatenate([part_of(even, k), part_of(swapped, k)], 0) for k in range(chunks)]
     last = [order]
-    pieces = {}
+    mine, theirs, gathered = {}, {}, {}
 
     def event(value):
         last[0] = after(value, last[0])
         return last[0]
 
-    def chunk(k):
-        held = packed[k]
-        if k:
-            held = other(held, k)
-            yield
-            held = event(held)
+    def gather(name, held):
         xs = [held]
         for _ in range(n - 1):
             held = step(held)
             yield
             held = event(held)
             xs.append(held)
-        hidden, part = hidden_of(order, xs, wg, wu, wd)
+        gathered[name] = xs
+
+    def arrive(k):
+        held = other(packed[k], k)
+        yield
+        gathered[k] = [event(held)]
+
+    def layer(k):
+        hidden, part = hidden_of(order, gathered[k], wg, wu, wd)
+        last[0] = part
         for j in (*range(2, n), 0):
             part = step(part)
             yield
@@ -163,22 +245,44 @@
             part = other(part, k)
             yield
             part = event(part)
-        theirs = sibling(part[capacity:])
+        mine[k] = part
+        back = sibling(part[capacity:])
         yield
-        pieces[k] = [part[:capacity], event(theirs)]
-
-    ways = [chunk(k) for k in range(chunks)]
+        theirs[k] = event(back)
+
+    def whole(k):
+        if k:
+            yield from arrive(k)
+            yield from gather(k, gathered[k][0])
+        else:
+            yield from gather(k, packed[k])
+            yield
+        yield from layer(k)
+
+    def first_of_halves(k):
+        if k:
+            yield from arrive(k)
+            ways[chunks + 2 * k] = gather((k, 0), gathered[k][0][:capacity])
+            ways[chunks + 2 * k + 1] = gather((k, 1), gathered[k][0][capacity:])
+        else:
+            ways[chunks] = gather((0, 0), part_of(even, 0))
+            ways[chunks + 1] = gather((0, 1), part_of(swapped, 0))
+        next(ways[chunks + 2 * k])
+        next(ways[chunks + 2 * k + 1])
+        yield
+        gathered[k] = [jnp.concatenate(pair, 0) for pair in zip(gathered[k, 0], gathered[k, 1])]
+        yield from layer(k)
+
+    ways = {k: first_of_halves(k) if k in HALVES else whole(k) for k in range(chunks)}
     for k in range(chunks):
         next(ways[k])
     for turn, k in enumerate(turns_of(chunks)):
+        if turn == LOAD_AT:
+            order, wg, wu, wd = load(after(order, last[0]), wg, wu, wd)
+            last[0] = order
         with jax.named_scope("chunk%d" % k):
             next(ways[k], None)
-        if turn == 1:
-            order = last[0] = order_of(after(order, last[0]), wg, wu, wd)
-    assert len(pieces) == chunks
-    back = jnp.concatenate([piece for k in range(chunks) for piece in pieces[k]], 0)
-    picked = lax.dot_general(selector, back, (((0,), (0,)), ((), ())), preferred_element_type=jnp.float32)
-    return (picked * gate_score).astype(jnp.bfloat16)
+    return combine(ids, gate_score, [mine[k] for k in range(chunks)], [theirs[k] for k in range(chunks)])
 
 
 def plain_program(tokens, route, gate_score, w_gate, w_up, w_down, capacity):

time: 143 us -> 133 us (0.930)
  Pallas kernels: 22.9 us -> 28.3 us
  local copies, waits for them, and re-layouts: 7.22 us -> 2.05 us
  starting transfers between devices: 36.8 us -> 33.7 us
  matrix products: 2.94 us -> 0 us
  waiting for transfers between devices: 71.1 us -> 68.4 us
  other arithmetic: 1.86 us -> 0.19 us
    ppermute x24, waiting for transfers between devices: 48.2 us -> 35.9 us  [square_program(): step = lambda a: lax.ppermute(a, ('expert', 'blk'), perm)]
    ppermute x6, waiting for transfers between devices: 19.2 us -> 29.4 us  [square_program(): lax.ppermute(a, 'expert', [(i, i ^ 2 * k) for i in range(groups)])]
    pallas_call x1 -> x3, Pallas kernels: 1.14 us -> 6.47 us  [the longest x1 2.35 us: dispatch(): pl.pallas_call(lambda *refs: dispatch_kernel(capacity, *refs), in_specs=[...]
    unnamed x21 -> x12, local copies, waits for them, and re-layouts: 6.25 us -> 1.88 us
    ppermute x24, starting transfers between devices: 22.6 us -> 18.8 us  [square_program(): step = lambda a: lax.ppermute(a, ('expert', 'blk'), perm)]
    dot_general x2 -> x0, matrix products: 2.94 us -> none  [the longest x1 1.96 us: square_program(): lax.dot_general(selector, back, (((0,), (0,)), ((), ())), preferred_eleme...]
  transfers between devices with their start and end apart: 35 -> 35, of which waited for: 26 -> 26; matrix products, arithmetic and copies ran while one was open for 1% -> 0% of each run, Pallas kernels for 15% -> 17%
where the time goes in v4:
time: 133 us
  waiting for transfers between devices  68.4 us (51%)
  starting transfers between devices  33.7 us (25%)
  Pallas kernels  28.3 us (21%)
  local copies, waits for them, and re-layouts  2.05 us (2%)
    ppermute x24, waiting for transfers between devices, square_program(): step = lambda a: lax.ppermute(a, ('expert', 'blk'), perm)  35.9 us
    ppermute x6, waiting for transfers between devices, square_program(): lax.ppermute(a, 'expert', [(i, i ^ 2 * k) for i in range(groups)])  29.4 us
    ppermute x24, starting transfers between devices, square_program(): step = lambda a: lax.ppermute(a, ('expert', 'blk'), perm)  18.8 us
    ppermute x6, starting transfers between devices, square_program(): lax.ppermute(a, 'expert', [(i, i ^ 2 * k) for i in range(groups)])  13.6 us
    pallas_call x12, Pallas kernels, down_of(): pl.pallas_call(lambda *refs: down_kernel(j, *refs), in_specs=[SMEM] + [VM...  11.1 us
    pallas_call x4, Pallas kernels, hidden_of(): pl.pallas_call(hidden_kernel, in_specs=[SMEM] + [VMEM] * 7, out_specs=[VM...  10.7 us
    ppermute x5, waiting for transfers between devices, square_program(): lax.ppermute(a, 'expert', [(i, i ^ 1) for i in range(groups)])  3.08 us
  transfers between devices with their start and end apart: 35, of which 26 were waited for; matrix products, arithmetic and copies ran while one was open for 0% of the time, Pallas kernels for 17%

profile of v4, /device:TPU:0, one launch (start us, length us, event | category | flops | bytes accessed | tf_op | source)
XLA Modules:
  0.0 132.9 jit_solution(2737930052625653839)
XLA Ops:
  1.9 2.4 %shard_map.64 = (bf16[384,896]{1,0:T(8,128)(2,1)S(1)}, bf16[384,896]{1,0:T(8,128)(2,1)S(1)}, s32[1,512]{1,0:T(1,128)S(1)}, s32[4]{0:T(128)S(1)}) custom-call(s32[2]{0:T(128)S(1)} %pad_add_fusion.refs_0_, s32[1,512]{1,0:T(1,128)S(1)} %bitcast.11, bf16[512,896]{1,0:T(8,128)(2,1)S(1)} %copy-done.4), custom_call_target="tpu_custom_call" | custom-call | flops 99999997952 | bytes 1 | tf_op jit(solution)/shard_map/pallas_call | solution.py:83
  4.9 1.7 %collective-permute-done = bf16[384,896]{1,0:T(8,128)(2,1)S(1)} collective-permute-done((bf16[384,896]{1,0:T(8,128)(2,1)S(1)}, bf16[384,896]{1,0:T(8,128)(2,1)S(1)}, u32[]{:S(2)}, u32[]{:S(2)}) %collective-permute-start) | collective-permute-done | bytes 688160 | tf_op jit(solution)/shard_map/ppermute | solution.py:207
  6.7 2.9 %collective-permute-start.1 = (bf16[192,896]{1,0:T(8,128)(2,1)S(1)}, bf16[192,896]{1,0:T(8,128)(2,1)S(1)}, u32[]{:S(2)}, u32[]{:S(2)}) collective-permute-start(bf16[192,896]{1,0:T(8,128)(2,1)S(1)} %pad_maximum_fusion.x0), channel_id=1, source_target_pairs={{0,1},{1,3},{3,2},{2,0},{4,6},{5,4},{7,5},{6,7},{8,9},{9,11},{11,1... | collective-permute-start | bytes 1032200 | tf_op jit(solution)/shard_map/ppermute | solution.py:210
  9.7 3.7 %collective-permute-start.3 = (bf16[192,896]{1,0:T(8,128)(2,1)S(1)}, bf16[192,896]{1,0:T(8,128)(2,1)S(1)}, u32[]{:S(2)}, u32[]{:S(2)}) collective-permute-start(bf16[192,896]{1,0:T(8,128)(2,1)S(1)} %pad_maximum_fusion.1), channel_id=1, source_target_pairs={{0,24},{4,28},{8,16},{12,20},{16,8},{20,12},{24,0},{28,4},{1,25},{... | collective-permute-start | bytes 1032200 | tf_op jit(solution)/shard_map/ppermute | solution.py:208
  13.3 1.6 %collective-permute-done.1.x1 = bf16[192,896]{1,0:T(8,128)(2,1)S(1)} collective-permute-done((bf16[192,896]{1,0:T(8,128)(2,1)S(1)}, bf16[192,896]{1,0:T(8,128)(2,1)S(1)}, u32[]{:S(2)}, u32[]{:S(2)}) %collective-permute-start.1) | collective-permute-done | bytes 344096 | tf_op jit(solution)/shard_map/ppermute | solution.py:210
  14.9 2.0 %collective-permute-start.2 = (bf16[192,896]{1,0:T(8,128)(2,1)S(1)}, bf16[192,896]{1,0:T(8,128)(2,1)S(1)}, u32[]{:S(2)}, u32[]{:S(2)}) collective-permute-start(bf16[192,896]{1,0:T(8,128)(2,1)S(1)} %collective-permute-done.1.x1), channel_id=1, source_target_pairs={{0,1},{1,3},{3,2},{2,0},{4,6},{5,4},{7,5},{6,7},{8,9},{9,11},{11,1... | collective-permute-start | bytes 1032200 | tf_op jit(solution)/shard_map/chunk0/ppermute | solution.py:210
  16.9 1.6 %collective-permute-start.6 = (bf16[192,896]{1,0:T(8,128)(2,1)S(1)}, bf16[192,896]{1,0:T(8,128)(2,1)S(1)}, u32[]{:S(2)}, u32[]{:S(2)}) collective-permute-start(bf16[192,896]{1,0:T(8,128)(2,1)S(1)} %pad_maximum_fusion.3), channel_id=1, source_target_pairs={{0,8},{4,12},{8,0},{12,4},{16,24},{20,28},{24,16},{28,20},{1,9},{5... | collective-permute-start | bytes 1032200 | tf_op jit(solution)/shard_map/ppermute | solution.py:208
  18.5 3.7 %collective-permute-done.3.x0 = bf16[192,896]{1,0:T(8,128)(2,1)S(1)} collective-permute-done((bf16[192,896]{1,0:T(8,128)(2,1)S(1)}, bf16[192,896]{1,0:T(8,128)(2,1)S(1)}, u32[]{:S(2)}, u32[]{:S(2)}) %collective-permute-start.3) | collective-permute-done | bytes 344096 | tf_op jit(solution)/shard_map/ppermute | solution.py:208
  23.4 1.9 %shard_map.65 = (s32[4]{0:T(128)S(1)}, bf16[3584,512]{1,0:T(8,128)(2,1)S(1)}, bf16[3584,512]{1,0:T(8,128)(2,1)S(1)}, bf16[512,3584]{1,0:T(8,128)(2,1)S(1)}) custom-call(s32[4]{0:T(128)S(1)} %get-tuple-element.63.order, bf16[3584,512]{1,0:T(8,128)(2,1)S(1)} %bitcast.7, bf16[3584,512]{1,0:T(8,128)(2,1)S(1)} %bitcast.8, bf16[512,3584]{1,0:T(8,128)(2,1)S(1)} %bitcast.9), custom_call_target="tpu_custom_call" | custom-call | flops 1 | bytes 1 | tf_op jit(solution)/shard_map/pallas_call | solution.py:139
  25.3 3.6 %collective-permute-done.6.x0 = bf16[192,896]{1,0:T(8,128)(2,1)S(1)} collective-permute-done((bf16[192,896]{1,0:T(8,128)(2,1)S(1)}, bf16[192,896]{1,0:T(8,128)(2,1)S(1)}, u32[]{:S(2)}, u32[]{:S(2)}) %collective-permute-start.6) | collective-permute-done | bytes 344096 | tf_op jit(solution)/shard_map/ppermute | solution.py:208
  29.5 1.4 %collective-permute-start.9 = (bf16[192,896]{1,0:T(8,128)(2,1)S(1)}, bf16[192,896]{1,0:T(8,128)(2,1)S(1)}, u32[]{:S(2)}, u32[]{:S(2)}) collective-permute-start(bf16[192,896]{1,0:T(8,128)(2,1)S(1)} %collective-permute-done.8.x1), channel_id=1, source_target_pairs={{0,1},{1,3},{3,2},{2,0},{4,6},{5,4},{7,5},{6,7},{8,9},{9,11},{11,1... | collective-permute-start | bytes 1032200 | tf_op jit(solution)/shard_map/chunk3/ppermute | solution.py:210
  30.9 6.4 %collective-permute-start.5 = (bf16[192,896]{1,0:T(8,128)(2,1)S(1)}, bf16[192,896]{1,0:T(8,128)(2,1)S(1)}, u32[]{:S(2)}, u32[]{:S(2)}) collective-permute-start(bf16[192,896]{1,0:T(8,128)(2,1)S(1)} %pad_maximum_fusion.2), channel_id=1, source_target_pairs={{0,16},{4,20},{8,24},{12,28},{16,0},{20,4},{24,8},{28,12},{1,17},{... | collective-permute-start | bytes 1032200 | tf_op jit(solution)/shard_map/ppermute | solution.py:208
  37.4 1.5 %collective-permute-start.4 = (bf16[192,896]{1,0:T(8,128)(2,1)S(1)}, bf16[192,896]{1,0:T(8,128)(2,1)S(1)}, u32[]{:S(2)}, u32[]{:S(2)}) collective-permute-start(bf16[192,896]{1,0:T(8,128)(2,1)S(1)} %collective-permute-done.2.x2), channel_id=1, source_target_pairs={{0,1},{1,3},{3,2},{2,0},{4,6},{5,4},{7,5},{6,7},{8,9},{9,11},{11,1... | collective-permute-start | bytes 1032200 | tf_op jit(solution)/shard_map/chunk0/ppermute | solution.py:210
  40.4 1.4 %collective-permute-start.11 = (bf16[192,896]{1,0:T(8,128)(2,1)S(1)}, bf16[192,896]{1,0:T(8,128)(2,1)S(1)}, u32[]{:S(2)}, u32[]{:S(2)}) collective-permute-start(bf16[192,896]{1,0:T(8,128)(2,1)S(1)} %collective-permute-done.7.x1), channel_id=1, source_target_pairs={{0,1},{1,3},{3,2},{2,0},{4,6},{5,4},{7,5},{6,7},{8,9},{9,11},{11,1... | collective-permute-start | bytes 1032200 | tf_op jit(solution)/shard_map/chunk1/ppermute | solution.py:210
  41.8 11.0 %collective-permute-done.5.x0 = bf16[192,896]{1,0:T(8,128)(2,1)S(1)} collective-permute-done((bf16[192,896]{1,0:T(8,128)(2,1)S(1)}, bf16[192,896]{1,0:T(8,128)(2,1)S(1)}, u32[]{:S(2)}, u32[]{:S(2)}) %collective-permute-start.5) | collective-permute-done | bytes 344096 | tf_op jit(solution)/shard_map/ppermute | solution.py:208
  52.8 2.7 %chunk3.4 = (bf16[192,512]{1,0:T(8,128)(2,1)S(1)}, bf16[192,896]{1,0:T(8,128)(2,1)S(1)}) custom-call(s32[4]{0:T(128)S(1)} %get-tuple-element.64.order.refs_0_, bf16[192,896]{1,0:T(8,128)(2,1)S(1)} %collective-permute-done.3.x0, bf16[192,896]{1,0:T(8,128)(2,1)S(1)} %collective-permute-done.8.x1, bf16[192,896]{1,0:T(8,128)(2,1)S(1)} %collective-permute-done.9.x2, ...), custom_call_target="tpu_custom_call" | custom-call | flops 1 | bytes 1 | tf_op jit(solution)/shard_map/chunk3/pallas_call | solution.py:154
  56.1 3.9 %collective-permute-done.14.x1 = bf16[192,896]{1,0:T(8,128)(2,1)S(1)} collective-permute-done((bf16[192,896]{1,0:T(8,128)(2,1)S(1)}, bf16[192,896]{1,0:T(8,128)(2,1)S(1)}, u32[]{:S(2)}, u32[]{:S(2)}) %collective-permute-start.14) | collective-permute-done | bytes 344096 | tf_op jit(solution)/shard_map/chunk2/ppermute | solution.py:210
  60.6 3.1 %collective-permute-done.13.x3 = bf16[192,896]{1,0:T(8,128)(2,1)S(1)} collective-permute-done((bf16[192,896]{1,0:T(8,128)(2,1)S(1)}, bf16[192,896]{1,0:T(8,128)(2,1)S(1)}, u32[]{:S(2)}, u32[]{:S(2)}) %collective-permute-start.13) | collective-permute-done | bytes 344096 | tf_op jit(solution)/shard_map/chunk1/ppermute | solution.py:210
  63.8 2.7 %chunk1.4 = (bf16[192,512]{1,0:T(8,128)(2,1)S(1)}, bf16[192,896]{1,0:T(8,128)(2,1)S(1)}) custom-call(s32[4]{0:T(128)S(1)} %get-tuple-element.64.order.refs_0_, bf16[192,896]{1,0:T(8,128)(2,1)S(1)} %collective-permute-done.6.x0, bf16[192,896]{1,0:T(8,128)(2,1)S(1)} %collective-permute-done.7.x1, bf16[192,896]{1,0:T(8,128)(2,1)S(1)} %collective-permute-done.11.x2, ...), custom_call_target="tpu_custom_call" | custom-call | flops 1 | bytes 1 | tf_op jit(solution)/shard_map/chunk1/pallas_call | solution.py:154
  68.8 2.7 %chunk0.4 = (bf16[192,512]{1,0:T(8,128)(2,1)S(1)}, bf16[192,896]{1,0:T(8,128)(2,1)S(1)}) custom-call(s32[4]{0:T(128)S(1)} %get-tuple-element.64.order.refs_0_, bf16[192,896]{1,0:T(8,128)(2,1)S(1)} %pad_maximum_fusion.x0, bf16[192,896]{1,0:T(8,128)(2,1)S(1)} %collective-permute-done.1.x1, bf16[192,896]{1,0:T(8,128)(2,1)S(1)} %collective-permute-done.2.x2, ...), custom_call_target="tpu_custom_call" | custom-call | flops 1 | bytes 1 | tf_op jit(solution)/shard_map/chunk0/pallas_call | solution.py:154
  72.4 1.8 %collective-permute-start.21 = (bf16[192,896]{1,0:T(8,128)(2,1)S(1)}, bf16[192,896]{1,0:T(8,128)(2,1)S(1)}, u32[]{:S(2)}, u32[]{:S(2)}) collective-permute-start(bf16[192,896]{1,0:T(8,128)(2,1)S(1)} %chunk3.5), channel_id=1, source_target_pairs={{0,1},{1,3},{3,2},{2,0},{4,6},{5,4},{7,5},{6,7},{8,9},{9,11},{11,1... | collective-permute-start | bytes 1032200 | tf_op jit(solution)/shard_map/chunk3/ppermute | solution.py:210
  74.8 2.7 %chunk2.4 = (bf16[192,512]{1,0:T(8,128)(2,1)S(1)}, bf16[192,896]{1,0:T(8,128)(2,1)S(1)}) custom-call(s32[4]{0:T(128)S(1)} %get-tuple-element.64.order.refs_0_, bf16[192,896]{1,0:T(8,128)(2,1)S(1)} %collective-permute-done.5.x0, bf16[192,896]{1,0:T(8,128)(2,1)S(1)} %collective-permute-done.14.x1, bf16[192,896]{1,0:T(8,128)(2,1)S(1)} %collective-permute-done.16.x2, ...), custom_call_target="tpu_custom_call" | custom-call | flops 1 | bytes 1 | tf_op jit(solution)/shard_map/chunk2/pallas_call | solution.py:154
  79.9 2.3 %collective-permute-done.21.refs_2_ = bf16[192,896]{1,0:T(8,128)(2,1)S(1)} collective-permute-done((bf16[192,896]{1,0:T(8,128)(2,1)S(1)}, bf16[192,896]{1,0:T(8,128)(2,1)S(1)}, u32[]{:S(2)}, u32[]{:S(2)}) %collective-permute-start.21) | collective-permute-done | bytes 344096 | tf_op jit(solution)/shard_map/chunk3/ppermute | solution.py:210
  83.2 2.7 %collective-permute-done.20.refs_2_ = bf16[192,896]{1,0:T(8,128)(2,1)S(1)} collective-permute-done((bf16[192,896]{1,0:T(8,128)(2,1)S(1)}, bf16[192,896]{1,0:T(8,128)(2,1)S(1)}, u32[]{:S(2)}, u32[]{:S(2)}) %collective-permute-start.20) | collective-permute-done | bytes 344096 | tf_op jit(solution)/shard_map/chunk2/ppermute | solution.py:210
  86.9 2.7 %collective-permute-done.19.refs_2_ = bf16[192,896]{1,0:T(8,128)(2,1)S(1)} collective-permute-done((bf16[192,896]{1,0:T(8,128)(2,1)S(1)}, bf16[192,896]{1,0:T(8,128)(2,1)S(1)}, u32[]{:S(2)}, u32[]{:S(2)}) %collective-permute-start.19) | collective-permute-done | bytes 344096 | tf_op jit(solution)/shard_map/chunk1/ppermute | solution.py:210
  94.2 1.4 %collective-permute-start.28 = (bf16[192,896]{1,0:T(8,128)(2,1)S(1)}, bf16[192,896]{1,0:T(8,128)(2,1)S(1)}, u32[]{:S(2)}, u32[]{:S(2)}) collective-permute-start(bf16[192,896]{1,0:T(8,128)(2,1)S(1)} %chunk3.7), channel_id=1, source_target_pairs={{0,24},{4,28},{8,16},{12,20},{16,8},{20,12},{24,0},{28,4},{1,25},{... | collective-permute-start | bytes 1032200 | tf_op jit(solution)/shard_map/chunk3/ppermute | solution.py:208
  98.1 2.5 %collective-permute-done.22.refs_2_ = bf16[192,896]{1,0:T(8,128)(2,1)S(1)} collective-permute-done((bf16[192,896]{1,0:T(8,128)(2,1)S(1)}, bf16[192,896]{1,0:T(8,128)(2,1)S(1)}, u32[]{:S(2)}, u32[]{:S(2)}) %collective-permute-start.22) | collective-permute-done | bytes 344096 | tf_op jit(solution)/shard_map/chunk1/ppermute | solution.py:210
  101.6 2.7 %collective-permute-done.10.refs_2_ = bf16[192,896]{1,0:T(8,128)(2,1)S(1)} collective-permute-done((bf16[192,896]{1,0:T(8,128)(2,1)S(1)}, bf16[192,896]{1,0:T(8,128)(2,1)S(1)}, u32[]{:S(2)}, u32[]{:S(2)}) %collective-permute-start.10) | collective-permute-done | bytes 344096 | tf_op jit(solution)/shard_map/chunk0/ppermute | solution.py:210
  108.9 3.1 %collective-permute-done.26.refs_1_ = bf16[192,896]{1,0:T(8,128)(2,1)S(1)} collective-permute-done((bf16[192,896]{1,0:T(8,128)(2,1)S(1)}, bf16[192,896]{1,0:T(8,128)(2,1)S(1)}, u32[]{:S(2)}, u32[]{:S(2)}) %collective-permute-start.26) | collective-permute-done | bytes 344096 | tf_op jit(solution)/shard_map/chunk1/ppermute | solution.py:208
  114.2 6.6 %collective-permute-done.29.refs_2_ = bf16[192,896]{1,0:T(8,128)(2,1)S(1)} collective-permute-done((bf16[192,896]{1,0:T(8,128)(2,1)S(1)}, bf16[192,896]{1,0:T(8,128)(2,1)S(1)}, u32[]{:S(2)}, u32[]{:S(2)}) %collective-permute-start.29) | collective-permute-done | bytes 344096 | tf_op jit(solution)/shard_map/chunk0/ppermute | solution.py:210
  122.5 6.7 %collective-permute-done.30.refs_2_ = bf16[192,896]{1,0:T(8,128)(2,1)S(1)} collective-permute-done((bf16[192,896]{1,0:T(8,128)(2,1)S(1)}, bf16[192,896]{1,0:T(8,128)(2,1)S(1)}, u32[]{:S(2)}, u32[]{:S(2)}) %collective-permute-start.30) | collective-permute-done | bytes 344096 | tf_op jit(solution)/shard_map/chunk2/ppermute | solution.py:208
  130.7 2.2 %shard_map.66 = bf16[512,896]{1,0:T(8,128)(2,1)} custom-call(s32[1,512]{1,0:T(1,128)S(1)} %get-tuple-element.56.ids, f32[1,512]{1,0:T(1,128)S(1)} %bitcast.10, bf16[192,896]{1,0:T(8,128)(2,1)S(1)} %chunk0.7.refs_0_, bf16[192,896]{1,0:T(8,128)(2,1)S(1)} %collective-permute-done.26.refs_1_, bf16[192,896]{1,0:T(8,128)(2,1)S(1)} %collective-permute-done.30.refs_2_, ...), custom_call_target="tpu_custom_call" | custom-call | flops 1 | bytes 1 | tf_op jit(solution)/shard_map/pallas_call | solution.py:114
  (80 shorter events, 33.4 us)
Async XLA Ops:
  6.7 8.2 %collective-permute-start.1 = (bf16[192,896]{1,0:T(8,128)(2,1)S(1)}, bf16[192,896]{1,0:T(8,128)(2,1)S(1)}, u32[]{:S(2)}, u32[]{:S(2)}) collective-permute-start(bf16[192,896]{1,0:T(8,128)(2,1)S(1)} %pad_maximum_fusion.x0), channel_id=1, source_target_pairs={{0,1},{1,3},{3,2},{2,0},{4,6},{5,4},{7,5},{6,7},{8,9},{9,11},{11,1... | collective-permute-start | bytes 1032200 | tf_op jit(solution)/shard_map/ppermute | solution.py:210
  9.7 12.6 %collective-permute-start.3 = (bf16[192,896]{1,0:T(8,128)(2,1)S(1)}, bf16[192,896]{1,0:T(8,128)(2,1)S(1)}, u32[]{:S(2)}, u32[]{:S(2)}) collective-permute-start(bf16[192,896]{1,0:T(8,128)(2,1)S(1)} %pad_maximum_fusion.1), channel_id=1, source_target_pairs={{0,24},{4,28},{8,16},{12,20},{16,8},{20,12},{24,0},{28,4},{1,25},{... | collective-permute-start | bytes 1032200 | tf_op jit(solution)/shard_map/ppermute | solution.py:208
  14.9 8.5 %collective-permute-start.2 = (bf16[192,896]{1,0:T(8,128)(2,1)S(1)}, bf16[192,896]{1,0:T(8,128)(2,1)S(1)}, u32[]{:S(2)}, u32[]{:S(2)}) collective-permute-start(bf16[192,896]{1,0:T(8,128)(2,1)S(1)} %collective-permute-done.1.x1), channel_id=1, source_target_pairs={{0,1},{1,3},{3,2},{2,0},{4,6},{5,4},{7,5},{6,7},{8,9},{9,11},{11,1... | collective-permute-start | bytes 1032200 | tf_op jit(solution)/shard_map/chunk0/ppermute | solution.py:210
  16.9 12.0 %collective-permute-start.6 = (bf16[192,896]{1,0:T(8,128)(2,1)S(1)}, bf16[192,896]{1,0:T(8,128)(2,1)S(1)}, u32[]{:S(2)}, u32[]{:S(2)}) collective-permute-start(bf16[192,896]{1,0:T(8,128)(2,1)S(1)} %pad_maximum_fusion.3), channel_id=1, source_target_pairs={{0,8},{4,12},{8,0},{12,4},{16,24},{20,28},{24,16},{28,20},{1,9},{5... | collective-permute-start | bytes 1032200 | tf_op jit(solution)/shard_map/ppermute | solution.py:208
  22.3 7.2 %collective-permute-start.8 = (bf16[192,896]{1,0:T(8,128)(2,1)S(1)}, bf16[192,896]{1,0:T(8,128)(2,1)S(1)}, u32[]{:S(2)}, u32[]{:S(2)}) collective-permute-start(bf16[192,896]{1,0:T(8,128)(2,1)S(1)} %collective-permute-done.3.x0), channel_id=1, source_target_pairs={{0,1},{1,3},{3,2},{2,0},{4,6},{5,4},{7,5},{6,7},{8,9},{9,11},{11,1... | collective-permute-start | bytes 1032200 | tf_op jit(solution)/shard_map/chunk3/ppermute | solution.py:210
  28.9 11.5 %collective-permute-start.7 = (bf16[192,896]{1,0:T(8,128)(2,1)S(1)}, bf16[192,896]{1,0:T(8,128)(2,1)S(1)}, u32[]{:S(2)}, u32[]{:S(2)}) collective-permute-start(bf16[192,896]{1,0:T(8,128)(2,1)S(1)} %collective-permute-done.6.x0), channel_id=1, source_target_pairs={{0,1},{1,3},{3,2},{2,0},{4,6},{5,4},{7,5},{6,7},{8,9},{9,11},{11,1... | collective-permute-start | bytes 1032200 | tf_op jit(solution)/shard_map/chunk1/ppermute | solution.py:210
  29.5 10.3 %collective-permute-start.9 = (bf16[192,896]{1,0:T(8,128)(2,1)S(1)}, bf16[192,896]{1,0:T(8,128)(2,1)S(1)}, u32[]{:S(2)}, u32[]{:S(2)}) collective-permute-start(bf16[192,896]{1,0:T(8,128)(2,1)S(1)} %collective-permute-done.8.x1), channel_id=1, source_target_pairs={{0,1},{1,3},{3,2},{2,0},{4,6},{5,4},{7,5},{6,7},{8,9},{9,11},{11,1... | collective-permute-start | bytes 1032200 | tf_op jit(solution)/shard_map/chunk3/ppermute | solution.py:210
  30.9 21.9 %collective-permute-start.5 = (bf16[192,896]{1,0:T(8,128)(2,1)S(1)}, bf16[192,896]{1,0:T(8,128)(2,1)S(1)}, u32[]{:S(2)}, u32[]{:S(2)}) collective-permute-start(bf16[192,896]{1,0:T(8,128)(2,1)S(1)} %pad_maximum_fusion.2), channel_id=1, source_target_pairs={{0,16},{4,20},{8,24},{12,28},{16,0},{20,4},{24,8},{28,12},{1,17},{... | collective-permute-start | bytes 1032200 | tf_op jit(solution)/shard_map/ppermute | solution.py:208
  37.4 15.4 %collective-permute-start.4 = (bf16[192,896]{1,0:T(8,128)(2,1)S(1)}, bf16[192,896]{1,0:T(8,128)(2,1)S(1)}, u32[]{:S(2)}, u32[]{:S(2)}) collective-permute-start(bf16[192,896]{1,0:T(8,128)(2,1)S(1)} %collective-permute-done.2.x2), channel_id=1, source_target_pairs={{0,1},{1,3},{3,2},{2,0},{4,6},{5,4},{7,5},{6,7},{8,9},{9,11},{11,1... | collective-permute-start | bytes 1032200 | tf_op jit(solution)/shard_map/chunk0/ppermute | solution.py:210
  39.8 13.0 %collective-permute-start.12 = (bf16[192,896]{1,0:T(8,128)(2,1)S(1)}, bf16[192,896]{1,0:T(8,128)(2,1)S(1)}, u32[]{:S(2)}, u32[]{:S(2)}) collective-permute-start(bf16[192,896]{1,0:T(8,128)(2,1)S(1)} %collective-permute-done.9.x2), channel_id=1, source_target_pairs={{0,1},{1,3},{3,2},{2,0},{4,6},{5,4},{7,5},{6,7},{8,9},{9,11},{11,1... | collective-permute-start | bytes 1032200 | tf_op jit(solution)/shard_map/chunk3/ppermute | solution.py:210
  40.4 15.1 %collective-permute-start.11 = (bf16[192,896]{1,0:T(8,128)(2,1)S(1)}, bf16[192,896]{1,0:T(8,128)(2,1)S(1)}, u32[]{:S(2)}, u32[]{:S(2)}) collective-permute-start(bf16[192,896]{1,0:T(8,128)(2,1)S(1)} %collective-permute-done.7.x1), channel_id=1, source_target_pairs={{0,1},{1,3},{3,2},{2,0},{4,6},{5,4},{7,5},{6,7},{8,9},{9,11},{11,1... | collective-permute-start | bytes 1032200 | tf_op jit(solution)/shard_map/chunk1/ppermute | solution.py:210
  52.8 7.2 %collective-permute-start.14 = (bf16[192,896]{1,0:T(8,128)(2,1)S(1)}, bf16[192,896]{1,0:T(8,128)(2,1)S(1)}, u32[]{:S(2)}, u32[]{:S(2)}) collective-permute-start(bf16[192,896]{1,0:T(8,128)(2,1)S(1)} %collective-permute-done.5.x0), channel_id=1, source_target_pairs={{0,1},{1,3},{3,2},{2,0},{4,6},{5,4},{7,5},{6,7},{8,9},{9,11},{11,1... | collective-permute-start | bytes 1032200 | tf_op jit(solution)/shard_map/chunk2/ppermute | solution.py:210
  55.5 8.2 %collective-permute-start.13 = (bf16[192,896]{1,0:T(8,128)(2,1)S(1)}, bf16[192,896]{1,0:T(8,128)(2,1)S(1)}, u32[]{:S(2)}, u32[]{:S(2)}) collective-permute-start(bf16[192,896]{1,0:T(8,128)(2,1)S(1)} %collective-permute-done.11.x2), channel_id=1, source_target_pairs={{0,1},{1,3},{3,2},{2,0},{4,6},{5,4},{7,5},{6,7},{8,9},{9,11},{11,1... | collective-permute-start | bytes 1032200 | tf_op jit(solution)/shard_map/chunk1/ppermute | solution.py:210
  60.1 7.4 %collective-permute-start.16 = (bf16[192,896]{1,0:T(8,128)(2,1)S(1)}, bf16[192,896]{1,0:T(8,128)(2,1)S(1)}, u32[]{:S(2)}, u32[]{:S(2)}) collective-permute-start(bf16[192,896]{1,0:T(8,128)(2,1)S(1)} %collective-permute-done.14.x1), channel_id=1, source_target_pairs={{0,1},{1,3},{3,2},{2,0},{4,6},{5,4},{7,5},{6,7},{8,9},{9,11},{11,1... | collective-permute-start | bytes 1032200 | tf_op jit(solution)/shard_map/chunk2/ppermute | solution.py:210
  60.1 11.4 %collective-permute-start.18 = (bf16[192,896]{1,0:T(8,128)(2,1)S(1)}, bf16[192,896]{1,0:T(8,128)(2,1)S(1)}, u32[]{:S(2)}, u32[]{:S(2)}) collective-permute-start(bf16[192,896]{1,0:T(8,128)(2,1)S(1)} %get-tuple-element.77), channel_id=1, source_target_pairs={{0,1},{1,3},{3,2},{2,0},{4,6},{5,4},{7,5},{6,7},{8,9},{9,11},{11,1... | collective-permute-start | bytes 1032200 | tf_op jit(solution)/shard_map/chunk3/ppermute | solution.py:210
  67.4 7.4 %collective-permute-start.17 = (bf16[192,896]{1,0:T(8,128)(2,1)S(1)}, bf16[192,896]{1,0:T(8,128)(2,1)S(1)}, u32[]{:S(2)}, u32[]{:S(2)}) collective-permute-start(bf16[192,896]{1,0:T(8,128)(2,1)S(1)} %collective-permute-done.16.x2), channel_id=1, source_target_pairs={{0,1},{1,3},{3,2},{2,0},{4,6},{5,4},{7,5},{6,7},{8,9},{9,11},{11,1... | collective-permute-start | bytes 1032200 | tf_op jit(solution)/shard_map/chunk2/ppermute | solution.py:210
  67.4 11.1 %collective-permute-start.15 = (bf16[192,896]{1,0:T(8,128)(2,1)S(1)}, bf16[192,896]{1,0:T(8,128)(2,1)S(1)}, u32[]{:S(2)}, u32[]{:S(2)}) collective-permute-start(bf16[192,896]{1,0:T(8,128)(2,1)S(1)} %get-tuple-element.82), channel_id=1, source_target_pairs={{0,1},{1,3},{3,2},{2,0},{4,6},{5,4},{7,5},{6,7},{8,9},{9,11},{11,1... | collective-permute-start | bytes 1032200 | tf_op jit(solution)/shard_map/chunk1/ppermute | solution.py:210
  72.4 9.8 %collective-permute-start.21 = (bf16[192,896]{1,0:T(8,128)(2,1)S(1)}, bf16[192,896]{1,0:T(8,128)(2,1)S(1)}, u32[]{:S(2)}, u32[]{:S(2)}) collective-permute-start(bf16[192,896]{1,0:T(8,128)(2,1)S(1)} %chunk3.5), channel_id=1, source_target_pairs={{0,1},{1,3},{3,2},{2,0},{4,6},{5,4},{7,5},{6,7},{8,9},{9,11},{11,1... | collective-permute-start | bytes 1032200 | tf_op jit(solution)/shard_map/chunk3/ppermute | solution.py:210
  77.5 8.4 %collective-permute-start.20 = (bf16[192,896]{1,0:T(8,128)(2,1)S(1)}, bf16[192,896]{1,0:T(8,128)(2,1)S(1)}, u32[]{:S(2)}, u32[]{:S(2)}) collective-permute-start(bf16[192,896]{1,0:T(8,128)(2,1)S(1)} %get-tuple-element.87), channel_id=1, source_target_pairs={{0,1},{1,3},{3,2},{2,0},{4,6},{5,4},{7,5},{6,7},{8,9},{9,11},{11,1... | collective-permute-start | bytes 1032200 | tf_op jit(solution)/shard_map/chunk2/ppermute | solution.py:210
  79.4 10.1 %collective-permute-start.19 = (bf16[192,896]{1,0:T(8,128)(2,1)S(1)}, bf16[192,896]{1,0:T(8,128)(2,1)S(1)}, u32[]{:S(2)}, u32[]{:S(2)}) collective-permute-start(bf16[192,896]{1,0:T(8,128)(2,1)S(1)} %chunk1.5), channel_id=1, source_target_pairs={{0,1},{1,3},{3,2},{2,0},{4,6},{5,4},{7,5},{6,7},{8,9},{9,11},{11,1... | collective-permute-start | bytes 1032200 | tf_op jit(solution)/shard_map/chunk1/ppermute | solution.py:210
  83.1 10.1 %collective-permute-start.24 = (bf16[192,896]{1,0:T(8,128)(2,1)S(1)}, bf16[192,896]{1,0:T(8,128)(2,1)S(1)}, u32[]{:S(2)}, u32[]{:S(2)}) collective-permute-start(bf16[192,896]{1,0:T(8,128)(2,1)S(1)} %chunk3.6), channel_id=1, source_target_pairs={{0,1},{1,3},{3,2},{2,0},{4,6},{5,4},{7,5},{6,7},{8,9},{9,11},{11,1... | collective-permute-start | bytes 1032200 | tf_op jit(solution)/shard_map/chunk3/ppermute | solution.py:210
  86.8 10.1 %collective-permute-start.23 = (bf16[192,896]{1,0:T(8,128)(2,1)S(1)}, bf16[192,896]{1,0:T(8,128)(2,1)S(1)}, u32[]{:S(2)}, u32[]{:S(2)}) collective-permute-start(bf16[192,896]{1,0:T(8,128)(2,1)S(1)} %chunk2.5), channel_id=1, source_target_pairs={{0,1},{1,3},{3,2},{2,0},{4,6},{5,4},{7,5},{6,7},{8,9},{9,11},{11,1... | collective-permute-start | bytes 1032200 | tf_op jit(solution)/shard_map/chunk2/ppermute | solution.py:210
  90.5 10.1 %collective-permute-start.22 = (bf16[192,896]{1,0:T(8,128)(2,1)S(1)}, bf16[192,896]{1,0:T(8,128)(2,1)S(1)}, u32[]{:S(2)}, u32[]{:S(2)}) collective-permute-start(bf16[192,896]{1,0:T(8,128)(2,1)S(1)} %chunk1.6), channel_id=1, source_target_pairs={{0,1},{1,3},{3,2},{2,0},{4,6},{5,4},{7,5},{6,7},{8,9},{9,11},{11,1... | collective-permute-start | bytes 1032200 | tf_op jit(solution)/shard_map/chunk1/ppermute | solution.py:210
  90.6 13.8 %collective-permute-start.10 = (bf16[192,896]{1,0:T(8,128)(2,1)S(1)}, bf16[192,896]{1,0:T(8,128)(2,1)S(1)}, u32[]{:S(2)}, u32[]{:S(2)}) collective-permute-start(bf16[192,896]{1,0:T(8,128)(2,1)S(1)} %get-tuple-element.75), channel_id=1, source_target_pairs={{0,1},{1,3},{3,2},{2,0},{4,6},{5,4},{7,5},{6,7},{8,9},{9,11},{11,1... | collective-permute-start | bytes 1032200 | tf_op jit(solution)/shard_map/chunk0/ppermute | solution.py:210
  94.2 12.5 %collective-permute-start.28 = (bf16[192,896]{1,0:T(8,128)(2,1)S(1)}, bf16[192,896]{1,0:T(8,128)(2,1)S(1)}, u32[]{:S(2)}, u32[]{:S(2)}) collective-permute-start(bf16[192,896]{1,0:T(8,128)(2,1)S(1)} %chunk3.7), channel_id=1, source_target_pairs={{0,24},{4,28},{8,16},{12,20},{16,8},{20,12},{24,0},{28,4},{1,25},{... | collective-permute-start | bytes 1032200 | tf_op jit(solution)/shard_map/chunk3/ppermute | solution.py:208
  97.9 10.1 %collective-permute-start.27 = (bf16[192,896]{1,0:T(8,128)(2,1)S(1)}, bf16[192,896]{1,0:T(8,128)(2,1)S(1)}, u32[]{:S(2)}, u32[]{:S(2)}) collective-permute-start(bf16[192,896]{1,0:T(8,128)(2,1)S(1)} %chunk2.6), channel_id=1, source_target_pairs={{0,1},{1,3},{3,2},{2,0},{4,6},{5,4},{7,5},{6,7},{8,9},{9,11},{11,1... | collective-permute-start | bytes 1032200 | tf_op jit(solution)/shard_map/chunk2/ppermute | solution.py:210
  101.6 10.5 %collective-permute-start.26 = (bf16[192,896]{1,0:T(8,128)(2,1)S(1)}, bf16[192,896]{1,0:T(8,128)(2,1)S(1)}, u32[]{:S(2)}, u32[]{:S(2)}) collective-permute-start(bf16[192,896]{1,0:T(8,128)(2,1)S(1)} %chunk1.7), channel_id=1, source_target_pairs={{0,8},{4,12},{8,0},{12,4},{16,24},{20,28},{24,16},{28,20},{1,9},{5... | collective-permute-start | bytes 1032200 | tf_op jit(solution)/shard_map/chunk1/ppermute | solution.py:208
  105.2 7.3 %collective-permute-start.25 = (bf16[192,896]{1,0:T(8,128)(2,1)S(1)}, bf16[192,896]{1,0:T(8,128)(2,1)S(1)}, u32[]{:S(2)}, u32[]{:S(2)}) collective-permute-start(bf16[192,896]{1,0:T(8,128)(2,1)S(1)} %chunk0.5), channel_id=1, source_target_pairs={{0,1},{1,3},{3,2},{2,0},{4,6},{5,4},{7,5},{6,7},{8,9},{9,11},{11,1... | collective-permute-start | bytes 1032200 | tf_op jit(solution)/shard_map/chunk0/ppermute | solution.py:210
  113.5 7.3 %collective-permute-start.29 = (bf16[192,896]{1,0:T(8,128)(2,1)S(1)}, bf16[192,896]{1,0:T(8,128)(2,1)S(1)}, u32[]{:S(2)}, u32[]{:S(2)}) collective-permute-start(bf16[192,896]{1,0:T(8,128)(2,1)S(1)} %chunk0.6), channel_id=1, source_target_pairs={{0,1},{1,3},{3,2},{2,0},{4,6},{5,4},{7,5},{6,7},{8,9},{9,11},{11,1... | collective-permute-start | bytes 1032200 | tf_op jit(solution)/shard_map/chunk0/ppermute | solution.py:210
  113.8 15.4 %collective-permute-start.30 = (bf16[192,896]{1,0:T(8,128)(2,1)S(1)}, bf16[192,896]{1,0:T(8,128)(2,1)S(1)}, u32[]{:S(2)}, u32[]{:S(2)}) collective-permute-start(bf16[192,896]{1,0:T(8,128)(2,1)S(1)} %chunk2.7), channel_id=1, source_target_pairs={{0,16},{4,20},{8,24},{12,28},{16,0},{20,4},{24,8},{28,12},{1,17},{... | collective-permute-start | bytes 1032200 | tf_op jit(solution)/shard_map/chunk2/ppermute | solution.py:208
  121.7 7.5 %collective-permute-start.31 = (bf16[96,896]{1,0:T(8,128)(2,1)S(1)}, bf16[96,896]{1,0:T(8,128)(2,1)S(1)}, u32[]{:S(2)}, u32[]{:S(2)}) collective-permute-start(bf16[96,896]{1,0:T(8,128)(2,1)S(1)} %slice.52), channel_id=1, source_target_pairs={{0,4},{4,0},{8,12},{12,8},{16,20},{20,16},{24,28},{28,24},{1,5},{5... | collective-permute-start | bytes 516104 | tf_op jit(solution)/shard_map/chunk0/ppermute | solution.py:207
  121.8 7.4 %collective-permute-start.32 = (bf16[96,896]{1,0:T(8,128)(2,1)S(1)}, bf16[96,896]{1,0:T(8,128)(2,1)S(1)}, u32[]{:S(2)}, u32[]{:S(2)}) collective-permute-start(bf16[96,896]{1,0:T(8,128)(2,1)S(1)} %slice.45), channel_id=1, source_target_pairs={{0,4},{4,0},{8,12},{12,8},{16,20},{20,16},{24,28},{28,24},{1,5},{5... | collective-permute-start | bytes 516104 | tf_op jit(solution)/shard_map/chunk1/ppermute | solution.py:207
  (9 other events, 91.6 us)
